TPU v7x, 1024 devices: a whole 4x4x32 slice. The times are simulated.
1024 devices in a mesh: gx: 8 (over y, core), gy: 8 (over z_hi, x), gz: 16 (over z_lo).
Axes of the slice: x: 4, y: 4, z: 32 (z_hi: 2, z_lo: 16; z = z_hi * 16 + z_lo), core: 2. Of those that a mesh axis runs over, the one named last changes fastest.
Arguments:
- node_feats: bfloat16 [8, 16, 32, 128, 128], P('gx', 'gy', 'gz'), may hold values from -6 to 6
- offsets: bfloat16 [8, 16, 32, 3, 128], P('gx', 'gy', 'gz'), may hold values from 0 to 1
- counts: int32 [8, 16, 32], P('gx', 'gy', 'gz'), may hold values from 0 to 128, as said below
- neighbours: int32 [8, 16, 32, 128, 8], P('gx', 'gy', 'gz'), may hold values from 0 to 3455, as said below
- pair_counts: int32 [8, 16, 32, 128], P('gx', 'gy', 'gz'), may hold values from 4 to 8
- radial_in: float32 [8, 64], replicated, may hold values from -2 to 2
- radial_out: bfloat16 [64, 384], replicated, may hold values from -0.75 to 0.75
- mix_weight: bfloat16 [512, 128], replicated, may hold values from -0.25 to 0.25
Outputs:
- updated: bfloat16 [8, 16, 32, 128, 128], P('gx', 'gy', 'gz')
Inputs may be any that keep to these rules, and one draw needn't show every extreme that they name: `counts`: bins whose third index lies outside 32 // 4 to 23 are empty; the others hold at least 32 atoms, and some bin holds 128. `neighbours`: for an atom slot of a bin that holds atoms, every entry names an occupied slot of a bin that holds atoms among the 27 bins around it (digit 13 is the bin itself).
All inputs are finite; a program needn't handle non-finite values.
Results may differ from a plain program's by a relative error of at most 0.0081.
Values may be sent and summed in bfloat16 or wider, within the bound.
A program may use at most 32 MiB of HBM per device.

v0:
```python
import math

import jax
import jax.numpy as jnp
from jax import lax
from jax.sharding import PartitionSpec as P

ROOT_THREE = math.sqrt(3.0)
ROOT_FIVE = math.sqrt(5.0)
ROOT_FIFTEEN = math.sqrt(15.0)
CUTOFF_BINS = 3.0
FLOOR_BINS = 0.25


def with_halo(value, sides, width):
    for axis, dim in sides:
        devices, length = (lax.axis_size(axis), value.shape[dim])
        up = [(i, (i + 1) % devices) for i in range(devices)]
        down = [(j, i) for i, j in up]
        last = lax.slice_in_dim(value, length - width, length, axis=dim)
        initial = lax.slice_in_dim(value, 0, width, axis=dim)
        before = lax.ppermute(last, axis, up)
        after = lax.ppermute(initial, axis, down)
        value = jnp.concatenate([before, value, after], axis=dim)
    return value


def bin_update(
    near_feats, near_offs, neighbour_rows, pair_count, atom_count, radial_in, radial_out, mix_weight
):
    slot_total = near_feats.shape[3]
    channels = near_feats.shape[4]
    pair_width = neighbour_rows.shape[1]
    flat_index = neighbour_rows.reshape(-1)
    gathered = jnp.take(near_feats.reshape(27 * slot_total, channels), flat_index, axis=0)
    flat_offs = (
        jnp.transpose(near_offs, (3, 0, 1, 2, 4)).reshape(3, 27 * slot_total).astype(jnp.float32)
    )
    their_offs = jnp.take(flat_offs, flat_index, axis=1)
    own_offs = jnp.repeat(near_offs[1, 1, 1].astype(jnp.float32), pair_width, axis=1)
    bin_digit = flat_index // slot_total
    bin_shift = jnp.stack([bin_digit // 9 - 1, bin_digit // 3 % 3 - 1, bin_digit % 3 - 1]).astype(
        jnp.float32
    )
    displace = bin_shift + their_offs - own_offs
    distance = jnp.sqrt(jnp.sum(displace * displace, axis=0))
    floored = jnp.maximum(distance, FLOOR_BINS)
    scaled = jnp.minimum(distance / CUTOFF_BINS, 1.0)
    envelope = 1.0 - 10.0 * scaled**3 + 15.0 * scaled**4 - 6.0 * scaled**5
    orders = jnp.arange(1, radial_in.shape[0] + 1).astype(jnp.float32)[:, None]
    basis = jnp.sin(math.pi * orders * scaled[None, :]) * (envelope / floored)[None, :]
    hidden = jax.nn.silu(jnp.dot(radial_in.T, basis, precision=lax.Precision.HIGHEST)).astype(
        jnp.bfloat16
    )
    radial = lax.dot_general(
        hidden, radial_out, (((0,), (0,)), ((), ())), preferred_element_type=jnp.float32
    ).astype(jnp.bfloat16)
    unit_vec = displace / floored[None, :]
    unit_x = unit_vec[0]
    unit_y = unit_vec[1]
    unit_z = unit_vec[2]
    harmonic = jnp.stack(
        [
            jnp.ones_like(unit_x),
            ROOT_THREE * unit_x,
            ROOT_THREE * unit_y,
            ROOT_THREE * unit_z,
            ROOT_FIFTEEN * unit_x * unit_y,
            ROOT_FIFTEEN * unit_y * unit_z,
            ROOT_FIFTEEN * unit_z * unit_x,
            0.5 * ROOT_FIVE * (3.0 * unit_z * unit_z - 1.0),
            0.5 * ROOT_FIFTEEN * (unit_x * unit_x - unit_y * unit_y),
        ]
    )
    pair_mask = (
        (jnp.arange(pair_width)[None, :] < pair_count[:, None]).astype(jnp.float32).reshape(-1)
    )
    weighted = (harmonic * pair_mask[None, :] * pair_width ** (-0.5)).reshape(
        9, slot_total, pair_width
    )
    amp_list = []
    for order, (first_row, last_row) in enumerate(((0, 1), (1, 4), (4, 9))):
        product = radial[:, order * channels : (order + 1) * channels].astype(
            jnp.float32
        ) * gathered.astype(jnp.float32)
        product = product.reshape(slot_total, pair_width, channels)
        comps = []
        for row in range(first_row, last_row):
            comps.append(jnp.sum(weighted[row][:, :, None] * product, axis=1))
        amp_list.append(jnp.stack(comps))
    scalar_part = amp_list[0][0].astype(jnp.bfloat16)
    vector_norm = jnp.sum(amp_list[1] * amp_list[1], axis=0).astype(jnp.bfloat16)
    tensor_norm = jnp.sum(amp_list[2] * amp_list[2], axis=0).astype(jnp.bfloat16)
    joined = jnp.concatenate([near_feats[1, 1, 1], scalar_part, vector_norm, tensor_norm], axis=1)
    mixed_rows = jnp.dot(joined, mix_weight, preferred_element_type=jnp.float32)
    live_slot = (jnp.arange(slot_total) < atom_count)[:, None]
    return jnp.where(live_slot, mixed_rows, 0.0).astype(jnp.bfloat16)


def run_bin(
    feats_ext, offs_ext, lists, pairs, sizes, pos_x, pos_y, pos_z, radial_in, radial_out, mix_weight
):
    near_feats = feats_ext[pos_x : pos_x + 3, pos_y : pos_y + 3, pos_z : pos_z + 3]
    near_offs = offs_ext[pos_x : pos_x + 3, pos_y : pos_y + 3, pos_z : pos_z + 3]
    atom_count = sizes[pos_x, pos_y, pos_z]

    def compute():
        return bin_update(
            near_feats,
            near_offs,
            lists[pos_x, pos_y, pos_z],
            pairs[pos_x, pos_y, pos_z],
            atom_count,
            radial_in,
            radial_out,
            mix_weight,
        )

    def nothing():
        return jnp.zeros(near_feats.shape[3:], jnp.bfloat16)

    return lax.cond(atom_count > 0, compute, nothing)


def bin_block(
    feats_ext, offs_ext, lists, pairs, sizes, z_first, z_last, radial_in, radial_out, mix_weight
):
    rows_y = []
    for pos_y in range(lists.shape[1]):
        rows_z = []
        for pos_z in range(z_first, z_last):
            rows_z.append(
                run_bin(
                    feats_ext,
                    offs_ext,
                    lists,
                    pairs,
                    sizes,
                    0,
                    pos_y,
                    pos_z,
                    radial_in,
                    radial_out,
                    mix_weight,
                )
            )
        rows_y.append(jnp.stack(rows_z))
    rows_x = [jnp.stack(rows_y)]
    return jnp.stack(rows_x)


def per_device(
    node_feats, offsets, counts, neighbours, pair_counts, radial_in, radial_out, mix_weight
):
    ext_feats, ext_offs = (
        with_halo(node_feats, (("gx", 0), ("gy", 1), ("gz", 2)), 1),
        with_halo(offsets, (("gx", 0), ("gy", 1), ("gz", 2)), 1),
    )
    depth_z = counts.shape[2]
    result = bin_block(
        ext_feats,
        ext_offs,
        neighbours,
        pair_counts,
        counts,
        0,
        depth_z,
        radial_in,
        radial_out,
        mix_weight,
    )
    return result


def solution(mesh):
    placed = (
        P("gx", "gy", "gz", None, None),
        P("gx", "gy", "gz", None, None),
        P("gx", "gy", "gz"),
        P("gx", "gy", "gz", None, None),
        P("gx", "gy", "gz", None),
        P(),
        P(),
        P(),
    )
    return jax.shard_map(
        per_device,
        mesh=mesh,
        in_specs=placed,
        out_specs=P("gx", "gy", "gz", None, None),
        check_vma=False,
    )
```

profile of v0, /device:TPU:128, one launch (start us, length us, event | category | flops | bytes accessed | tf_op | source)
XLA Modules:
  0.0 215.2 jit_solution(10963201351090091219)
XLA Ops:
  0.0 1.7 collective-permute-start
  1.7 1.3 collective-permute-start.1
  3.5 1.0 collective-permute-done.5
  5.9 0.9 constant_dynamic-update-slice_fusion.1
  6.9 26.4 %collective-permute-start.3 = (bf16[3,1,2,128,128]{4,3,2,1,0:T(8,128)(2,1)S(1)}, bf16[3,1,2,128,128]{4,3,2,1,0:T(8,128)(2,1)S(1)}, u32[]{:S(2)}, u32[]{:S(2)}) collective-permute-start(bf16[3,1,2,128,128]{4,3,2,1,0:T(8,128)(2,1)S(1)} %get-tuple-element.464), channel_id=1, source_target_pairs={{16,0},{32,16},{48,32},{64,48},{80,64},{96,80},{112,96},{0,112},{1... | collective-permute-start | bytes 589832 | tf_op jit(solution)/shard_map/ppermute | solution.py:23
  33.2 1.9 collective-permute-start.2
  35.2 24.4 %collective-permute-start.8 = (bf16[3,1,2,3,128]{4,2,3,1,0:T(2,128)(2,1)S(1)}, bf16[3,1,2,3,128]{4,2,3,1,0:T(2,128)(2,1)S(1)}, u32[]{:S(2)}, u32[]{:S(2)}) collective-permute-start(bf16[3,1,2,3,128]{4,2,3,1,0:T(2,128)(2,1)S(1)} %get-tuple-element.470), channel_id=1, source_target_pairs={{16,0},{32,16},{48,32},{64,48},{80,64},{96,80},{112,96},{0,112},{1... | collective-permute-start | bytes 13832 | tf_op jit(solution)/shard_map/ppermute | solution.py:23
  59.5 1.9 collective-permute-start.7
  61.5 6.8 %collective-permute-done.8 = bf16[3,1,2,3,128]{4,2,3,1,0:T(2,128)(2,1)S(1)} collective-permute-done((bf16[3,1,2,3,128]{4,2,3,1,0:T(2,128)(2,1)S(1)}, bf16[3,1,2,3,128]{4,2,3,1,0:T(2,128)(2,1)S(1)}, u32[]{:S(2)}, u32[]{:S(2)}) %collective-permute-start.8) | collective-permute-done | bytes 4640 | tf_op jit(solution)/shard_map/ppermute | solution.py:23
  68.3 25.3 %collective-permute-done.7 = bf16[3,1,2,3,128]{4,2,3,1,0:T(2,128)(2,1)S(1)} collective-permute-done((bf16[3,1,2,3,128]{4,2,3,1,0:T(2,128)(2,1)S(1)}, bf16[3,1,2,3,128]{4,2,3,1,0:T(2,128)(2,1)S(1)}, u32[]{:S(2)}, u32[]{:S(2)}) %collective-permute-start.7) | collective-permute-done | bytes 4640 | tf_op jit(solution)/shard_map/ppermute | solution.py:22
  93.9 1.9 collective-permute-start.4
  95.8 5.1 %collective-permute-start.10 = (bf16[3,4,1,128,128]{4,3,2,1,0:T(8,128)(2,1)S(1)}, bf16[3,4,1,128,128]{4,3,2,1,0:T(8,128)(2,1)}, u32[]{:S(2)}, u32[]{:S(2)}) collective-permute-start(bf16[3,4,1,128,128]{4,3,2,1,0:T(8,128)(2,1)S(1)} %get-tuple-element.462), channel_id=1, source_target_pairs={{1,0},{2,1},{3,2},{4,3},{5,4},{6,5},{7,6},{8,7},{9,8},{10,9},{11,1... | collective-permute-start | bytes 1179656 | tf_op jit(solution)/shard_map/ppermute | solution.py:23
  101.0 1.9 collective-permute-start.9
  102.9 5.1 %collective-permute-start.11 = (bf16[3,4,1,3,128]{4,1,3,2,0:T(4,128)(2,1)S(1)}, bf16[3,4,1,3,128]{4,1,3,2,0:T(4,128)(2,1)S(1)}, u32[]{:S(2)}, u32[]{:S(2)}) collective-permute-start(bf16[3,4,1,3,128]{4,1,3,2,0:T(4,128)(2,1)S(1)} %get-tuple-element.468), channel_id=1, source_target_pairs={{1,0},{2,1},{3,2},{4,3},{5,4},{6,5},{7,6},{8,7},{9,8},{10,9},{11,1... | collective-permute-start | bytes 27656 | tf_op jit(solution)/shard_map/ppermute | solution.py:23
  111.3 6.0 %collective-permute-done.11 = bf16[3,4,1,3,128]{4,1,3,2,0:T(4,128)(2,1)S(1)} collective-permute-done((bf16[3,4,1,3,128]{4,1,3,2,0:T(4,128)(2,1)S(1)}, bf16[3,4,1,3,128]{4,1,3,2,0:T(4,128)(2,1)S(1)}, u32[]{:S(2)}, u32[]{:S(2)}) %collective-permute-start.11) | collective-permute-done | bytes 9248 | tf_op jit(solution)/shard_map/ppermute | solution.py:23
  117.9 1.2 maximum_maximum_fusion
  119.1 25.9 %conditional.5 = (bf16[1,128,128]{2,1,0:T(8,128)(2,1)S(1)}) conditional(s32[]{:T(128)} %convert_element_type.281, () %tuple.41, (s32[]{:T(128)}, bf16[3,4,3,128,128]{4,3,2,1,0:T(8,128)(2,1)S(1)}, s32[1,2,2,128,8]{3,4,2,1,0:T(8,128)S(1)}, bf16[3,4,3,3,128]{4,1,3,2,0:T(4,128)(2,1)}, s32[1,2,2,128]{3,2,1,0:T(2,128)}, /*index=5*/f32[8,64]{1,0:T(8,128)}, ...), branch_computations={%region_14.17_spmd, %region_15.30_spmd} | conditional | flops 78427800 | bytes 8245808 | solution.py:122
  119.2 1.4 copy.254
  121.2 1.5 copy.243
  122.7 1.5 broadcast_in_dim.82
  124.2 1.7 reshape.1099
  125.9 1.4 slice_convert_fusion.1
  128.1 4.3 %gather_fusion.2 = f32[1024,3]{1,0:T(8,128)S(1)} fusion(f32[3,3456]{0,1:T(8,128)} %bitcast.290, s32[1024]{0:T(1024)S(1)} %fusion.78), kind=kCustom, calls=%fused_computation.2.clone | custom fusion | bytes 28672 | tf_op jit(solution)/shard_map/cond/branch_1_fun/jit(_take)/gather | solution.py:39
  133.5 1.3 convolution_convert_fusion.1
  136.7 3.2 %gather_fusion.3 = bf16[1024,128]{1,0:T(8,128)(2,1)S(1)} fusion(bf16[3456,128]{1,0:T(8,128)(2,1)S(1)} %bitcast.286, s32[1024]{0:T(1024)S(1)} %copy-done.17), kind=kCustom, calls=%fused_computation.5.clone | custom fusion | bytes 528384 | tf_op jit(solution)/shard_map/cond/branch_1_fun/jit(_take)/gather | solution.py:35
  140.7 3.3 %fusion.44 = (bf16[128,128]{1,0:T(8,128)(2,1)S(1)}, f32[128,128]{1,0:T(8,128)S(1)}, f32[128,128]{1,0:T(8,128)S(1)}, f32[128,128]{1,0:T(8,128)S(1)}, f32[128,128]...) fusion(bf16[1024,384]{1,0:T(8,128)(2,1)} %convolution_convert_f, ...), kind=kLoop, calls=%fused_computation.124 | loop fusion | flops 3260416 | bytes 1643520 | tf_op jit(solution)/shard_map/cond/branch_1_fun/reduce_sum | solution.py:89
  145.7 24.7 %conditional.4 = (bf16[1,128,128]{2,1,0:T(8,128)(2,1)S(1)}) conditional(s32[]{:T(128)} %convert_element_type.280, () %tuple.39, (s32[]{:T(128)}, bf16[3,4,3,128,128]{4,3,2,1,0:T(8,128)(2,1)S(1)}, s32[1,2,2,128,8]{3,4,2,1,0:T(8,128)}, bf16[3,4,3,3,128]{4,1,3,2,0:T(4,128)(2,1)}, s32[1,2,2,128]{3,2,1,0:T(2,128)}, /*index=5*/f32[8,64]{1,0:T(8,128)}, ...), branch_computations={%region_0.0_spmd, %region_1.16_spmd} | conditional | flops 78427800 | bytes 8311372 | solution.py:122
  145.7 1.4 copy.252
  149.5 1.7 reshape.1094
  151.1 1.4 slice_convert_fusion
  153.4 4.3 %gather_fusion = f32[1024,3]{1,0:T(8,128)S(1)} fusion(f32[3,3456]{0,1:T(8,128)} %bitcast.291, s32[1024]{0:T(1024)S(1)} %fusion.38), kind=kCustom, calls=%fused_computation.clone | custom fusion | bytes 28672 | tf_op jit(solution)/shard_map/cond/branch_1_fun/jit(_take)/gather | solution.py:39
  158.8 1.3 convolution_convert_fusion
  162.0 3.2 %gather_fusion.1 = bf16[1024,128]{1,0:T(8,128)(2,1)S(1)} fusion(bf16[3456,128]{1,0:T(8,128)(2,1)S(1)} %bitcast.287, s32[1024]{0:T(1024)S(1)} %copy-done.19), kind=kCustom, calls=%fused_computation.1.clone | custom fusion | bytes 528384 | tf_op jit(solution)/shard_map/cond/branch_1_fun/jit(_take)/gather | solution.py:35
  165.9 3.3 %fusion.4 = (bf16[128,128]{1,0:T(8,128)(2,1)S(1)}, f32[128,128]{1,0:T(8,128)S(1)}, f32[128,128]{1,0:T(8,128)S(1)}, f32[128,128]{1,0:T(8,128)S(1)}, f32[128,128]{...) fusion(bf16[1024,384]{1,0:T(8,128)(2,1)} %convolution_convert_f, ...), kind=kLoop, calls=%fused_computation.19 | loop fusion | flops 3260416 | bytes 1643520 | tf_op jit(solution)/shard_map/cond/branch_1_fun/reduce_sum | solution.py:89
  170.9 24.7 %conditional.7 = (bf16[1,128,128]{2,1,0:T(8,128)(2,1)S(1)}) conditional(s32[]{:T(128)} %convert_element_type.283, () %tuple.45, (s32[]{:T(128)}, bf16[3,4,3,128,128]{4,3,2,1,0:T(8,128)(2,1)S(1)}, s32[1,2,2,128,8]{3,4,2,1,0:T(8,128)}, bf16[3,4,3,3,128]{4,1,3,2,0:T(4,128)(2,1)}, s32[1,2,2,128]{3,2,1,0:T(2,128)}, /*index=5*/f32[8,64]{1,0:T(8,128)}, ...), branch_computations={%region_42.45_spmd, %region_43.58_spmd} | conditional | flops 78427800 | bytes 8311372 | solution.py:122
  170.9 1.4 copy.258
  174.7 1.7 reshape.1109
  176.4 1.4 slice_convert_fusion.3
  178.7 4.3 %gather_fusion.6 = f32[1024,3]{1,0:T(8,128)S(1)} fusion(f32[3,3456]{0,1:T(8,128)} %bitcast.292, s32[1024]{0:T(1024)S(1)} %fusion.158), kind=kCustom, calls=%fused_computation.4.clone | custom fusion | bytes 28672 | tf_op jit(solution)/shard_map/cond/branch_1_fun/jit(_take)/gather | solution.py:39
  184.1 1.3 convolution_convert_fusion.3
  187.3 3.2 %gather_fusion.7 = bf16[1024,128]{1,0:T(8,128)(2,1)S(1)} fusion(bf16[3456,128]{1,0:T(8,128)(2,1)S(1)} %bitcast.288, s32[1024]{0:T(1024)S(1)} %copy-done.21), kind=kCustom, calls=%fused_computation.7.clone | custom fusion | bytes 528384 | tf_op jit(solution)/shard_map/cond/branch_1_fun/jit(_take)/gather | solution.py:35
  191.2 3.3 %fusion.124 = (bf16[128,128]{1,0:T(8,128)(2,1)S(1)}, f32[128,128]{1,0:T(8,128)S(1)}, f32[128,128]{1,0:T(8,128)S(1)}, f32[128,128]{1,0:T(8,128)S(1)}, f32[128,128...) fusion(bf16[1024,384]{1,0:T(8,128)(2,1)} %convolution_convert_f, ...), kind=kLoop, calls=%fused_computation.334 | loop fusion | flops 3260416 | bytes 1643520 | tf_op jit(solution)/shard_map/cond/branch_1_fun/reduce_sum | solution.py:89
  196.2 17.5 %conditional.6 = (bf16[1,128,128]{2,1,0:T(8,128)(2,1)S(1)}) conditional(s32[]{:T(128)} %convert_element_type.282, () %tuple.43, (s32[]{:T(128)}, bf16[3,4,3,128,128]{4,3,2,1,0:T(8,128)(2,1)S(1)}, s32[1,2,2,128,8]{3,4,2,1,0:T(8,128)}, bf16[3,4,3,3,128]{4,1,3,2,0:T(4,128)(2,1)}, s32[1,2,2,128]{3,2,1,0:T(2,128)}, /*index=5*/f32[8,64]{1,0:T(8,128)}, ...), branch_computations={%region_28.31_spmd, %region_29.44_spmd} | conditional | flops 78427800 | bytes 8221120 | solution.py:122
  196.2 1.4 copy.256
  198.0 1.4 slice_convert_fusion.2
  199.7 4.3 %gather_fusion.4 = f32[1024,3]{1,0:T(8,128)S(1)} fusion(f32[3,3456]{0,1:T(8,128)} %bitcast.293, s32[1024]{0:T(1024)S(1)} %fusion.118), kind=kCustom, calls=%fused_computation.3.clone | custom fusion | bytes 28672 | tf_op jit(solution)/shard_map/cond/branch_1_fun/jit(_take)/gather | solution.py:39
  206.8 3.2 %gather_fusion.5 = bf16[1024,128]{1,0:T(8,128)(2,1)S(1)} fusion(bf16[3456,128]{1,0:T(8,128)(2,1)S(1)} %bitcast.289, s32[1024]{0:T(1024)S(1)} %fusion.118), kind=kCustom, calls=%fused_computation.6.clone | custom fusion | bytes 528384 | tf_op jit(solution)/shard_map/cond/branch_1_fun/jit(_take)/gather | solution.py:35
  210.7 1.9 fusion.84
  (282 shorter events, 33.2 us)
Async XLA Ops:
  0.0 4.4 %collective-permute-start.5 = (bf16[1,2,2,3,128]{4,2,3,1,0:T(2,128)(2,1)}, bf16[1,2,2,3,128]{4,2,3,1,0:T(2,128)(2,1)S(1)}, u32[]{:S(2)}, u32[]{:S(2)}) collective-permute-start(bf16[1,2,2,3,128]{4,2,3,1,0:T(2,128)(2,1)} %param.21), channel_id=1, source_target_pairs={{0,128},{128,256},{256,384},{384,512},{512,640},{640,768},{768,896... | collective-permute-start | bytes 9224 | tf_op jit(solution)/shard_map/ppermute | solution.py:22
  0.0 5.8 %collective-permute-start = (bf16[1,2,2,128,128]{4,3,2,1,0:T(8,128)(2,1)}, bf16[1,2,2,128,128]{4,3,2,1,0:T(8,128)(2,1)S(1)}, u32[]{:S(2)}, u32[]{:S(2)}) collective-permute-start(bf16[1,2,2,128,128]{4,3,2,1,0:T(8,128)(2,1)} %param.20), channel_id=1, source_target_pairs={{0,128},{128,256},{256,384},{384,512},{512,640},{640,768},{768,896... | collective-permute-start | bytes 393224 | tf_op jit(solution)/shard_map/ppermute | solution.py:22
  1.7 5.1 %collective-permute-start.1 = (bf16[1,2,2,128,128]{4,3,2,1,0:T(8,128)(2,1)}, bf16[1,2,2,128,128]{4,3,2,1,0:T(8,128)(2,1)S(1)}, u32[]{:S(2)}, u32[]{:S(2)}) collective-permute-start(bf16[1,2,2,128,128]{4,3,2,1,0:T(8,128)(2,1)} %param.20), channel_id=1, source_target_pairs={{128,0},{256,128},{384,256},{512,384},{640,512},{768,640},{896,768... | collective-permute-start | bytes 393224 | tf_op jit(solution)/shard_map/ppermute | solution.py:23
  3.0 2.8 %collective-permute-start.6 = (bf16[1,2,2,3,128]{4,2,3,1,0:T(2,128)(2,1)}, bf16[1,2,2,3,128]{4,2,3,1,0:T(2,128)(2,1)S(1)}, u32[]{:S(2)}, u32[]{:S(2)}) collective-permute-start(bf16[1,2,2,3,128]{4,2,3,1,0:T(2,128)(2,1)} %param.21), channel_id=1, source_target_pairs={{128,0},{256,128},{384,256},{512,384},{640,512},{768,640},{896,768... | collective-permute-start | bytes 9224 | tf_op jit(solution)/shard_map/ppermute | solution.py:23
  6.9 86.8 %collective-permute-start.3 = (bf16[3,1,2,128,128]{4,3,2,1,0:T(8,128)(2,1)S(1)}, bf16[3,1,2,128,128]{4,3,2,1,0:T(8,128)(2,1)S(1)}, u32[]{:S(2)}, u32[]{:S(2)}) collective-permute-start(bf16[3,1,2,128,128]{4,3,2,1,0:T(8,128)(2,1)S(1)} %get-tuple-element.464), channel_id=1, source_target_pairs={{16,0},{32,16},{48,32},{64,48},{80,64},{96,80},{112,96},{0,112},{1... | collective-permute-start | bytes 589832 | tf_op jit(solution)/shard_map/ppermute | solution.py:23
  33.2 60.4 %collective-permute-start.2 = (bf16[3,1,2,128,128]{4,3,2,1,0:T(8,128)(2,1)S(1)}, bf16[3,1,2,128,128]{4,3,2,1,0:T(8,128)(2,1)S(1)}, u32[]{:S(2)}, u32[]{:S(2)}) collective-permute-start(bf16[3,1,2,128,128]{4,3,2,1,0:T(8,128)(2,1)S(1)} %get-tuple-element.463), channel_id=1, source_target_pairs={{0,16},{16,32},{32,48},{48,64},{64,80},{80,96},{96,112},{112,0},{1... | collective-permute-start | bytes 589832 | tf_op jit(solution)/shard_map/ppermute | solution.py:22
  35.2 33.1 %collective-permute-start.8 = (bf16[3,1,2,3,128]{4,2,3,1,0:T(2,128)(2,1)S(1)}, bf16[3,1,2,3,128]{4,2,3,1,0:T(2,128)(2,1)S(1)}, u32[]{:S(2)}, u32[]{:S(2)}) collective-permute-start(bf16[3,1,2,3,128]{4,2,3,1,0:T(2,128)(2,1)S(1)} %get-tuple-element.470), channel_id=1, source_target_pairs={{16,0},{32,16},{48,32},{64,48},{80,64},{96,80},{112,96},{0,112},{1... | collective-permute-start | bytes 13832 | tf_op jit(solution)/shard_map/ppermute | solution.py:23
  59.5 34.1 %collective-permute-start.7 = (bf16[3,1,2,3,128]{4,2,3,1,0:T(2,128)(2,1)S(1)}, bf16[3,1,2,3,128]{4,2,3,1,0:T(2,128)(2,1)S(1)}, u32[]{:S(2)}, u32[]{:S(2)}) collective-permute-start(bf16[3,1,2,3,128]{4,2,3,1,0:T(2,128)(2,1)S(1)} %get-tuple-element.469), channel_id=1, source_target_pairs={{0,16},{16,32},{32,48},{48,64},{64,80},{80,96},{96,112},{112,0},{1... | collective-permute-start | bytes 13832 | tf_op jit(solution)/shard_map/ppermute | solution.py:22
  93.8 14.2 %copy-start.28 = (s32[1,2,2]{2,1,0:T(2,128)S(1)}, s32[1,2,2]{2,1,0:T(2,128)}, u32[]{:S(2)}) copy-start(s32[1,2,2]{2,1,0:T(2,128)} %param.22) | copy-start | bytes 52
  93.9 24.1 %collective-permute-start.4 = (bf16[3,4,1,128,128]{4,3,2,1,0:T(8,128)(2,1)S(1)}, bf16[3,4,1,128,128]{4,3,2,1,0:T(8,128)(2,1)S(1)}, u32[]{:S(2)}, u32[]{:S(2)}) collective-permute-start(bf16[3,4,1,128,128]{4,3,2,1,0:T(8,128)(2,1)S(1)} %get-tuple-element.461), channel_id=1, source_target_pairs={{0,1},{1,2},{2,3},{3,4},{4,5},{5,6},{6,7},{7,8},{8,9},{9,10},{10,1... | collective-permute-start | bytes 1179656 | tf_op jit(solution)/shard_map/ppermute | solution.py:22
  95.8 22.1 %collective-permute-start.10 = (bf16[3,4,1,128,128]{4,3,2,1,0:T(8,128)(2,1)S(1)}, bf16[3,4,1,128,128]{4,3,2,1,0:T(8,128)(2,1)}, u32[]{:S(2)}, u32[]{:S(2)}) collective-permute-start(bf16[3,4,1,128,128]{4,3,2,1,0:T(8,128)(2,1)S(1)} %get-tuple-element.462), channel_id=1, source_target_pairs={{1,0},{2,1},{3,2},{4,3},{5,4},{6,5},{7,6},{8,7},{9,8},{10,9},{11,1... | collective-permute-start | bytes 1179656 | tf_op jit(solution)/shard_map/ppermute | solution.py:23
  101.0 10.3 %collective-permute-start.9 = (bf16[3,4,1,3,128]{4,1,3,2,0:T(4,128)(2,1)S(1)}, bf16[3,4,1,3,128]{4,1,3,2,0:T(4,128)(2,1)S(1)}, u32[]{:S(2)}, u32[]{:S(2)}) collective-permute-start(bf16[3,4,1,3,128]{4,1,3,2,0:T(4,128)(2,1)S(1)} %get-tuple-element.467), channel_id=1, source_target_pairs={{0,1},{1,2},{2,3},{3,4},{4,5},{5,6},{6,7},{7,8},{8,9},{9,10},{10,1... | collective-permute-start | bytes 27656 | tf_op jit(solution)/shard_map/ppermute | solution.py:22
  102.9 14.4 %collective-permute-start.11 = (bf16[3,4,1,3,128]{4,1,3,2,0:T(4,128)(2,1)S(1)}, bf16[3,4,1,3,128]{4,1,3,2,0:T(4,128)(2,1)S(1)}, u32[]{:S(2)}, u32[]{:S(2)}) collective-permute-start(bf16[3,4,1,3,128]{4,1,3,2,0:T(4,128)(2,1)S(1)} %get-tuple-element.468), channel_id=1, source_target_pairs={{1,0},{2,1},{3,2},{4,3},{5,4},{6,5},{7,6},{8,7},{9,8},{10,9},{11,1... | collective-permute-start | bytes 27656 | tf_op jit(solution)/shard_map/ppermute | solution.py:23
  117.9 1.2 copy-start.4
  127.3 5.6 %copy-start.13 = (f32[3,1024]{1,0:T(4,128)S(1)}, f32[3,1024]{1,0:T(4,128)}, u32[]{:S(2)}) copy-start(f32[3,1024]{1,0:T(4,128)} %reshape.1099) | copy-start | bytes 36868 | tf_op jit(solution)/shard_map/cond
  127.3 5.6 %copy-start.33 = (f32[8,64]{1,0:T(8,128)S(1)}, f32[8,64]{1,0:T(8,128)}, u32[]{:S(2)}) copy-start(f32[8,64]{1,0:T(8,128)} %get-tuple-element.100) | copy-start | bytes 6148 | tf_op jit(solution)/shard_map/cond
  127.4 6.1 %copy-start = (bf16[64,384]{1,0:T(8,128)(2,1)S(1)}, bf16[64,384]{1,0:T(8,128)(2,1)}, u32[]{:S(2)}) copy-start(bf16[64,384]{1,0:T(8,128)(2,1)} %get-tuple-element.101) | copy-start | bytes 147460 | tf_op jit(solution)/shard_map/cond
  127.5 0.6 copy-start.16
  132.6 2.2 %copy-start.22 = (pred[1024]{0:T(1024)(128)(4,1)}, pred[1024]{0:T(1024)(128)(4,1)S(1)}, u32[]{:S(2)}) copy-start(pred[1024]{0:T(1024)(128)(4,1)S(1)} %compare_and_fusion.1) | copy-start | bytes 3076 | tf_op jit(solution)/shard_map/cond
  134.8 1.9 copy-start.17
  136.7 3.9 %copy-start.23 = (pred[1024]{0:T(1024)(128)(4,1)S(1)}, pred[1024]{0:T(1024)(128)(4,1)}, u32[]{:S(2)}) copy-start(pred[1024]{0:T(1024)(128)(4,1)} %copy-done.22) | copy-start | bytes 3076 | tf_op jit(solution)/shard_map/cond
  144.0 0.9 copy-start.29
  145.1 0.6 copy-start.8
  151.1 1.4 copy-start.5
  152.5 5.6 %copy-start.14 = (f32[3,1024]{1,0:T(4,128)S(1)}, f32[3,1024]{1,0:T(4,128)}, u32[]{:S(2)}) copy-start(f32[3,1024]{1,0:T(4,128)} %reshape.1094) | copy-start | bytes 36868 | tf_op jit(solution)/shard_map/cond
  152.5 5.6 %copy-start.34 = (f32[8,64]{1,0:T(8,128)S(1)}, f32[8,64]{1,0:T(8,128)}, u32[]{:S(2)}) copy-start(f32[8,64]{1,0:T(8,128)} %get-tuple-element.92) | copy-start | bytes 6148 | tf_op jit(solution)/shard_map/cond
  152.7 6.1 %copy-start.1 = (bf16[64,384]{1,0:T(8,128)(2,1)S(1)}, bf16[64,384]{1,0:T(8,128)(2,1)}, u32[]{:S(2)}) copy-start(bf16[64,384]{1,0:T(8,128)(2,1)} %get-tuple-element.93) | copy-start | bytes 147460 | tf_op jit(solution)/shard_map/cond
  157.9 2.2 %copy-start.24 = (pred[1024]{0:T(1024)(128)(4,1)}, pred[1024]{0:T(1024)(128)(4,1)S(1)}, u32[]{:S(2)}) copy-start(pred[1024]{0:T(1024)(128)(4,1)S(1)} %compare_and_fusion) | copy-start | bytes 3076 | tf_op jit(solution)/shard_map/cond
  160.1 1.9 copy-start.19
  162.0 3.9 %copy-start.25 = (pred[1024]{0:T(1024)(128)(4,1)S(1)}, pred[1024]{0:T(1024)(128)(4,1)}, u32[]{:S(2)}) copy-start(pred[1024]{0:T(1024)(128)(4,1)} %copy-done.24) | copy-start | bytes 3076 | tf_op jit(solution)/shard_map/cond
  169.2 0.9 copy-start.30
  170.3 0.6 copy-start.10
  176.4 1.4 copy-start.6
  177.8 5.6 %copy-start.15 = (f32[3,1024]{1,0:T(4,128)S(1)}, f32[3,1024]{1,0:T(4,128)}, u32[]{:S(2)}) copy-start(f32[3,1024]{1,0:T(4,128)} %reshape.1109) | copy-start | bytes 36868 | tf_op jit(solution)/shard_map/cond
  177.8 5.7 %copy-start.35 = (f32[8,64]{1,0:T(8,128)S(1)}, f32[8,64]{1,0:T(8,128)}, u32[]{:S(2)}) copy-start(f32[8,64]{1,0:T(8,128)} %get-tuple-element.116) | copy-start | bytes 6148 | tf_op jit(solution)/shard_map/cond
  178.0 6.1 %copy-start.2 = (bf16[64,384]{1,0:T(8,128)(2,1)S(1)}, bf16[64,384]{1,0:T(8,128)(2,1)}, u32[]{:S(2)}) copy-start(bf16[64,384]{1,0:T(8,128)(2,1)} %get-tuple-element.117) | copy-start | bytes 147460 | tf_op jit(solution)/shard_map/cond
  178.1 0.6 copy-start.20
  183.2 2.2 %copy-start.26 = (pred[1024]{0:T(1024)(128)(4,1)}, pred[1024]{0:T(1024)(128)(4,1)S(1)}, u32[]{:S(2)}) copy-start(pred[1024]{0:T(1024)(128)(4,1)S(1)} %compare_and_fusion.3) | copy-start | bytes 3076 | tf_op jit(solution)/shard_map/cond
  185.4 1.9 copy-start.21
  187.3 3.9 %copy-start.27 = (pred[1024]{0:T(1024)(128)(4,1)S(1)}, pred[1024]{0:T(1024)(128)(4,1)}, u32[]{:S(2)}) copy-start(pred[1024]{0:T(1024)(128)(4,1)} %copy-done.26) | copy-start | bytes 3076 | tf_op jit(solution)/shard_map/cond
  194.5 0.9 copy-start.31
  195.6 0.6 copy-start.12
  195.6 18.1 %copy-start.9 = (bf16[1,128,128]{2,1,0:T(8,128)(2,1)S(1)}, bf16[1,128,128]{2,1,0:T(8,128)(2,1)}, u32[]{:S(2)}) copy-start(bf16[1,128,128]{2,1,0:T(8,128)(2,1)} %copy-done.8) | copy-start | bytes 98308
  195.6 18.1 %copy-start.11 = (bf16[1,128,128]{2,1,0:T(8,128)(2,1)S(1)}, bf16[1,128,128]{2,1,0:T(8,128)(2,1)}, u32[]{:S(2)}) copy-start(bf16[1,128,128]{2,1,0:T(8,128)(2,1)} %copy-done.10) | copy-start | bytes 98308
  198.0 1.4 copy-start.7
  199.4 5.1 %copy-start.36 = (f32[8,64]{1,0:T(8,128)S(1)}, f32[8,64]{1,0:T(8,128)}, u32[]{:S(2)}) copy-start(f32[8,64]{1,0:T(8,128)} %get-tuple-element.108) | copy-start | bytes 6148 | tf_op jit(solution)/shard_map/cond
  199.5 5.5 %copy-start.3 = (bf16[64,384]{1,0:T(8,128)(2,1)S(1)}, bf16[64,384]{1,0:T(8,128)(2,1)}, u32[]{:S(2)}) copy-start(bf16[64,384]{1,0:T(8,128)(2,1)} %get-tuple-element.109) | copy-start | bytes 147460 | tf_op jit(solution)/shard_map/cond
  212.6 0.9 copy-start.32
  (1 other events, 0.6 us)
where the time goes:
time: 217 us; the launch traced here: 215 us
  starting transfers between devices  72.1 us (33%)
  local copies, waits for them, and re-layouts  64.9 us (30%)
  waiting for transfers between devices  39.8 us (18%)
  other arithmetic  26.8 us (12%)
  matrix products  7.18 us (3%)
  between operations  2.84 us (1%)
    ppermute x6, starting transfers between devices, with_halo(): after = lax.ppermute(initial, axis, down)  62.8 us
    ppermute x6, waiting for transfers between devices, with_halo(): before = lax.ppermute(last, axis, up)  26.3 us
    gather x8, local copies, waits for them, and re-layouts, bin_update(): their_offs = jnp.take(flat_offs, flat_index, axis=1)  17.9 us
    ppermute x6, waiting for transfers between devices, with_halo(): after = lax.ppermute(initial, axis, down)  13.5 us
    gather x4, local copies, waits for them, and re-layouts, bin_update(): jnp.take(near_feats.reshape(27 * slot_total, channels), flat_index, axis=0)  12.8 us
    reduce_sum x4, other arithmetic, bin_update(): comps.append(jnp.sum(weighted[row][:, :, None] * product, axis=1))  11.8 us
    ppermute x6, starting transfers between devices, with_halo(): before = lax.ppermute(last, axis, up)  9.37 us
    another operation x12, local copies, waits for them, and re-layouts  6.13 us
  transfers between devices with their start and end apart: 12, of which 5 were waited for; matrix products, arithmetic and copies ran while one was open for 1% of the time, Pallas kernels for 0%

commit v1 on v0

v1 whole, which is shorter than its diff:
```python
import functools
import math

import jax
import jax.numpy as jnp
from jax import lax
from jax.experimental import pallas as pl
from jax.experimental.pallas import tpu as pltpu
from jax.sharding import PartitionSpec as P

ROOT_THREE = math.sqrt(3.0)
ROOT_FIVE = math.sqrt(5.0)
ROOT_FIFTEEN = math.sqrt(15.0)
CUTOFF_BINS = 3.0
FLOOR_BINS = 0.25
AXES = ("gx", "gy", "gz")
MESH = pl.DeviceIdType.MESH
AROUND = [(dx, dz) for dz in (-1, 0, 1) for dx in (-1, 0, 1) if (dx, dz) != (0, 0)]
BF16 = jnp.bfloat16
F32 = jnp.float32


def sin_pi(value):
    whole = jnp.floor(value + 0.5)
    r = value - whole
    odd = whole - 2.0 * jnp.floor(0.5 * whole)
    square = r * r
    total = jnp.full_like(r, -(math.pi**11) / math.factorial(11))
    for power in (9, 7, 5, 3, 1):
        sign = 1.0 if power % 4 == 1 else -1.0
        total = total * square + sign * math.pi**power / math.factorial(power)
    return (1.0 - 2.0 * odd) * r * total


def kernel(
    sizes,
    feats,
    offs,
    lists,
    pairs,
    counts,
    radial_in,
    radial_out,
    mix_weight,
    out,
    ext,
    places,
    hot_in,
    hot_out,
    halves,
    spread,
    radial,
    gathered,
    own_sem,
    send_sem,
    recv_sem,
):
    size_x, size_y, size_z = sizes
    me_x, me_y, me_z = (lax.axis_index(axis) for axis in AXES)
    z_first, z_last = size_z // 4, size_z // 4 + size_z // 2 - 1
    live = (me_z >= z_first) & (me_z <= z_last)
    below, above = me_z > z_first, me_z < z_last

    def has(dz):
        return {-1: below, 0: me_z >= 0, 1: above}[dz]

    def at(dx, dy, dz):
        return (
            lax.rem(me_x + dx + size_x, size_x),
            lax.rem(me_y + dy + size_y, size_y),
            lax.rem(me_z + dz + size_z, size_z),
        )

    def remote(number, source, target, device):
        return pltpu.make_async_remote_copy(
            src_ref=source,
            dst_ref=target,
            send_sem=send_sem.at[number],
            recv_sem=recv_sem.at[number],
            device_id=device,
            device_id_type=MESH,
        )

    z_from = {-1: pl.ds(0, 1), 0: pl.ds(0, 2), 1: pl.ds(1, 1)}
    z_from_ext = {-1: pl.ds(1, 1), 0: pl.ds(1, 2), 1: pl.ds(2, 1)}
    z_to = {-1: pl.ds(3, 1), 0: pl.ds(1, 2), 1: pl.ds(0, 1)}

    place_y = [
        remote(0, places.at[1, 1, 2], places.at[1, 1, 0], at(0, 1, 0)),
        remote(1, places.at[1, 1, 1], places.at[1, 1, 3], at(0, -1, 0)),
    ]
    feat_y = [
        remote(2, feats.at[0, 1], ext.at[1, 0, pl.ds(1, 2)], at(0, 1, 0)),
        remote(3, feats.at[0, 0], ext.at[1, 3, pl.ds(1, 2)], at(0, -1, 0)),
    ]
    place_around = [
        remote(4 + n, places.at[1, 1], places.at[1 - dx, 1 - dz], at(dx, 0, dz))
        for n, (dx, dz) in enumerate(AROUND)
    ]
    feat_own = [
        remote(
            12 + n,
            feats.at[0, pl.ds(0, 2), z_from[dz]],
            ext.at[1 - dx, pl.ds(1, 2), z_to[dz]],
            at(dx, 0, dz),
        )
        for n, (dx, dz) in enumerate(AROUND)
    ]

    def feat_relay(slot):
        row = 3 * slot
        return [
            remote(
                20 + 8 * slot + n,
                ext.at[1, row, z_from_ext[dz]],
                ext.at[1 - dx, row, z_to[dz]],
                at(dx, 0, dz),
            )
            for n, (dx, dz) in enumerate(AROUND)
        ]

    def start_around(copies):
        for (dx, dz), copy in zip(AROUND, copies):
            pl.when(has(dz))(copy.start)

    def recv_around(copies):
        for (dx, dz), copy in zip(AROUND, copies):
            pl.when(has(-dz))(copy.wait_recv)

    def send_around(copies):
        for (dx, dz), copy in zip(AROUND, copies):
            pl.when(has(dz))(copy.wait_send)

    def lists_of(b):
        hy, hz = b // 2, b % 2
        flat = lists[0, hy, hz]
        digit = flat >> 7
        step_x = (digit * 57) >> 9
        rest = digit - 9 * step_x
        step_y = (rest * 11) >> 5
        step_z = rest - 3 * step_y
        return flat & 127, digit, step_x, step_y, step_z

    lane = lax.broadcasted_iota(jnp.int32, (8, 128), 1)
    row = lax.broadcasted_iota(jnp.int32, (8, 128), 0)

    def one_hots(b):
        hy, hz = b // 2, b % 2
        slot, _, step_x, step_y, step_z = lists_of(b)
        used = row < pairs[0, hy, pl.ds(hz, 1), :]
        layer = step_y - 1 + hy
        inner = (layer == 0) | (layer == 1)
        around = step_x * 3 + step_z
        t_in = jnp.where(used & inner, around, -1)
        t_out = jnp.where(used & jnp.logical_not(inner), around, -1)
        slot_col = slot.astype(F32).T
        in_col = t_in.astype(F32).T
        out_col = t_out.astype(F32).T
        halves[b] = layer.astype(F32).T
        lanes = lax.broadcasted_iota(jnp.int32, (128, 128), 1).astype(F32).astype(BF16)
        zero = jnp.zeros((128, 128), BF16)
        for k in range(8):
            rows = pl.ds(128 * k, 128)

            def spread_col(col):
                return jnp.broadcast_to(col[:, k : k + 1], (128, 128)).astype(BF16)

            slots = jnp.where(spread_col(slot_col) == lanes, jnp.ones_like(zero), zero)
            in_k, out_k = spread_col(in_col), spread_col(out_col)
            for t in range(9):
                cols = pl.ds(128 * t, 128)
                hot_in[b, rows, cols] = jnp.where(in_k == float(t), slots, zero)
                hot_out[b, rows, cols] = jnp.where(out_k == float(t), slots, zero)

    def geometry(b):
        hy, hz = b // 2, b % 2
        slot, digit, step_x, step_y, step_z = lists_of(b)
        theirs = [jnp.zeros((8, 128), F32) for _ in range(3)]
        for d in range(27):
            dx, dy, dz = d // 9, d // 3 % 3, d % 3
            there = hz + dz
            chosen = digit == d
            for c in range(3):
                table = places[dx, (there + 1) // 2, hy + dy, pl.ds((there + 1) % 2 * 3 + c, 1), :]
                value = jnp.take_along_axis(jnp.broadcast_to(table, (8, 128)), slot, axis=1)
                theirs[c] = jnp.where(chosen, value, theirs[c])
        displace = []
        for c, step in enumerate((step_x, step_y, step_z)):
            own = places[1, 1, 1 + hy, pl.ds(hz * 3 + c, 1), :]
            displace.append((step - 1).astype(F32) + theirs[c] - own)
        x, y, z = displace
        distance = jnp.sqrt(x * x + y * y + z * z)
        floored = jnp.maximum(distance, FLOOR_BINS)
        u = jnp.minimum(distance / CUTOFF_BINS, 1.0)
        cube = u * u * u
        envelope = 1.0 - 10.0 * cube + 15.0 * cube * u - 6.0 * cube * u * u
        height = envelope / floored

        def along(value):
            return jnp.concatenate(
                [jnp.broadcast_to(value[k : k + 1, :], (8, 128)) for k in range(8)], axis=1
            )

        order = (lax.broadcasted_iota(jnp.int32, (8, 1024), 0) + 1).astype(F32)
        basis = sin_pi(order * along(u)) * along(height)
        before = jnp.dot(
            radial_in[...].T, basis, precision=lax.Precision.HIGHEST, preferred_element_type=F32
        )
        hidden = (0.5 * before * (1.0 + jnp.tanh(0.5 * before))).T.astype(BF16)
        radial[b] = jnp.dot(hidden, radial_out[...], preferred_element_type=F32).astype(BF16)

        pick = (row >> 1) * 32 + (lane & 31)
        k_here = (row & 1) * 4 + (lane >> 5)

        def regroup(value):
            total = jnp.zeros((8, 128), F32)
            for k in range(8):
                moved = jnp.take_along_axis(
                    jnp.broadcast_to(value[k : k + 1, :], (8, 128)), pick, axis=1
                )
                total = jnp.where(k_here == k, moved, total)
            return total

        x, y, z = (regroup(part / floored) for part in (x, y, z))
        harmonic = [
            ROOT_THREE * x,
            ROOT_THREE * y,
            ROOT_THREE * z,
            ROOT_FIFTEEN * x * y,
            ROOT_FIFTEEN * y * z,
            ROOT_FIFTEEN * z * x,
            0.5 * ROOT_FIVE * (3.0 * z * z - 1.0),
            0.5 * ROOT_FIFTEEN * (x * x - y * y),
        ]
        diagonal = (lax.broadcasted_iota(jnp.int32, (32, 128), 1) & 31) == (
            lax.broadcasted_iota(jnp.int32, (32, 128), 0)
        )
        for m in range(8):
            scaled = harmonic[m] * 8.0**-0.5
            for group in range(4):
                for part in range(2):
                    r = 2 * group + part
                    block = jnp.where(
                        diagonal, jnp.broadcast_to(scaled[r : r + 1, :], (32, 128)), 0.0
                    )
                    spread[b, group, pl.ds(32 * m, 32), pl.ds(128 * part, 128)] = block.astype(BF16)

    def gather_inner(b):
        hz = b % 2
        table = jnp.concatenate(
            [
                jnp.concatenate([ext[dx, 1, hz + dz], ext[dx, 2, hz + dz]], axis=1)
                for dx in range(3)
                for dz in range(3)
            ],
            axis=0,
        )
        both = jnp.dot(hot_in[b], table, preferred_element_type=F32)
        for k in range(8):
            part = both[128 * k : 128 * (k + 1)]
            upper = jnp.broadcast_to(halves[b, :, k : k + 1], (128, 128)) > 0.5
            gathered[b, pl.ds(128 * k, 128)] = jnp.where(upper, part[:, 128:], part[:, :128])

    def finish(b):
        hy, hz = b // 2, b % 2
        table = jnp.concatenate(
            [ext[dx, 3 * hy, hz + dz] for dx in range(3) for dz in range(3)], axis=0
        )
        theirs = gathered[b] + jnp.dot(hot_out[b], table, preferred_element_type=F32)
        first = radial[b, :, 0:128].astype(F32) * theirs
        total = first[0:128]
        for k in range(1, 8):
            total = total + first[128 * k : 128 * (k + 1)]
        scalar_part = (total * 8.0**-0.5).astype(BF16)
        vector = (radial[b, :, 128:256].astype(F32) * theirs).astype(BF16)
        tensor = (radial[b, :, 256:384].astype(F32) * theirs).astype(BF16)
        norms = [[], []]
        for group in range(4):
            for which, (product, first_m, last_m) in enumerate(((vector, 0, 3), (tensor, 3, 8))):
                part = jnp.concatenate(
                    [product[128 * k + 32 * group : 128 * k + 32 * group + 32] for k in range(8)],
                    axis=0,
                )
                amp = jnp.dot(
                    spread[b, group, pl.ds(32 * first_m, 32 * (last_m - first_m)), :],
                    part,
                    preferred_element_type=F32,
                )
                norm = None
                for m in range(last_m - first_m):
                    piece = amp[32 * m : 32 * (m + 1)]
                    norm = piece * piece if norm is None else norm + piece * piece
                norms[which].append(norm.astype(BF16))
        joined = jnp.concatenate(
            [
                ext[1, 1 + hy, 1 + hz],
                scalar_part,
                jnp.concatenate(norms[0], axis=0),
                jnp.concatenate(norms[1], axis=0),
            ],
            axis=1,
        )
        mixed = jnp.dot(joined, mix_weight[...], preferred_element_type=F32)
        live_slot = lax.broadcasted_iota(jnp.int32, (128, 128), 0) < counts[0, hy, hz]
        out[0, hy, hz] = jnp.where(live_slot, mixed, 0.0).astype(BF16)

    def each_bin(body):
        def step(b, carry):
            body(b)
            return carry

        lax.fori_loop(0, 4, step, 0)

    @pl.when(jnp.logical_not(live))
    def _():
        out[...] = jnp.zeros_like(out)

    @pl.when(live)
    def _():
        barrier = pltpu.get_barrier_semaphore()
        for dy in (-1, 1):
            pl.semaphore_signal(barrier, inc=1, device_id=at(0, dy, 0), device_id_type=MESH)
        for dx, dz in AROUND:

            @pl.when(has(dz))
            def _():
                pl.semaphore_signal(barrier, inc=1, device_id=at(dx, 0, dz), device_id_type=MESH)

        own_copy = pltpu.make_async_copy(feats.at[0], ext.at[1, pl.ds(1, 2), pl.ds(1, 2)], own_sem)
        own_copy.start()
        for y in range(2):
            for c in range(3):
                value = offs[0, y, c].astype(F32)
                for z in range(2):
                    places[1, 1, 1 + y, 3 * z + c : 3 * z + c + 1, :] = value[z : z + 1]
            places[1, 1, 1 + y, 6:8, :] = jnp.zeros((2, 128), F32)
        pl.semaphore_wait(
            barrier, 4 + 3 * below.astype(jnp.int32) + 3 * above.astype(jnp.int32)
        )
        for copy in place_y + feat_y:
            copy.start()
        start_around(feat_own)

        @pl.when(jnp.logical_not(below))
        def _():
            ext[:, :, 0] = jnp.zeros((3, 4, 128, 128), BF16)

        @pl.when(jnp.logical_not(above))
        def _():
            ext[:, :, 3] = jnp.zeros((3, 4, 128, 128), BF16)

        each_bin(one_hots)
        for copy in place_y:
            copy.wait_recv()
        start_around(place_around)
        early = lax.rem(me_y, 2)

        def relay(slot):
            feat_y[slot].wait_recv()
            start_around(feat_relay(slot))

        pl.when(early == 0)(functools.partial(relay, 1))
        pl.when(early == 1)(functools.partial(relay, 0))
        recv_around(place_around)
        each_bin(geometry)
        pl.when(early == 0)(functools.partial(relay, 0))
        pl.when(early == 1)(functools.partial(relay, 1))
        own_copy.wait()
        recv_around(feat_own)
        each_bin(gather_inner)
        recv_around(feat_relay(0))
        recv_around(feat_relay(1))
        each_bin(finish)
        for copy in place_y + feat_y:
            copy.wait_send()
        for copies in (place_around, feat_own, feat_relay(0), feat_relay(1)):
            send_around(copies)


def per_device(sizes, *arrays):
    node_feats, offsets, counts, neighbours, pair_counts, radial_in, radial_out, mix_weight = arrays
    vmem = pl.BlockSpec(memory_space=pltpu.VMEM)
    return pl.pallas_call(
        functools.partial(kernel, sizes),
        out_shape=jax.ShapeDtypeStruct(node_feats.shape, BF16),
        in_specs=[
            pl.BlockSpec(memory_space=pl.ANY),
            vmem,
            vmem,
            vmem,
            pl.BlockSpec(memory_space=pltpu.SMEM),
            vmem,
            vmem,
            vmem,
        ],
        out_specs=vmem,
        scratch_shapes=[
            pltpu.VMEM((3, 4, 4, 128, 128), BF16),
            pltpu.VMEM((3, 3, 4, 8, 128), F32),
            pltpu.VMEM((4, 1024, 1152), BF16),
            pltpu.VMEM((4, 1024, 1152), BF16),
            pltpu.VMEM((4, 128, 8), F32),
            pltpu.VMEM((4, 4, 256, 256), BF16),
            pltpu.VMEM((4, 1024, 384), BF16),
            pltpu.VMEM((4, 1024, 128), F32),
            pltpu.SemaphoreType.DMA,
            pltpu.SemaphoreType.DMA((36,)),
            pltpu.SemaphoreType.DMA((36,)),
        ],
        compiler_params=pltpu.CompilerParams(
            collective_id=0, has_side_effects=True, vmem_limit_bytes=50 * 1024 * 1024
        ),
        cost_estimate=pl.CostEstimate(
            flops=4_000_000_000, bytes_accessed=4_000_000, transcendentals=600_000
        ),
    )(
        node_feats,
        jnp.transpose(offsets, (0, 1, 3, 2, 4)),
        jnp.swapaxes(neighbours, 3, 4),
        pair_counts,
        counts,
        radial_in,
        radial_out,
        mix_weight,
    )


def solution(mesh):
    placed = (
        P("gx", "gy", "gz", None, None),
        P("gx", "gy", "gz", None, None),
        P("gx", "gy", "gz"),
        P("gx", "gy", "gz", None, None),
        P("gx", "gy", "gz", None),
        P(),
        P(),
        P(),
    )
    sizes = tuple(mesh.shape[axis] for axis in AXES)
    return jax.shard_map(
        functools.partial(per_device, sizes),
        mesh=mesh,
        in_specs=placed,
        out_specs=P("gx", "gy", "gz", None, None),
        check_vma=False,
    )
```

time: 217 us -> 62.3 us (0.29)
  the two profiles are of different devices: /device:TPU:128 before, /device:TPU:160 now
where the time goes in v1:
time: 62.3 us; the launch traced here: 61.9 us
  Pallas kernels  55.2 us (89%)
  local copies, waits for them, and re-layouts  6.71 us (11%)
    pallas_call x1, Pallas kernels, per_device(): pl.pallas_call(functools.partial(kernel, sizes), out_shape=jax.ShapeDtype...  55.2 us
    unnamed x17, local copies, waits for them, and re-layouts  6.71 us

profile of v1, /device:TPU:160, one launch (start us, length us, event | category | flops | bytes accessed | tf_op | source)
XLA Modules:
  0.0 61.9 jit_solution(16812054155294422880)
XLA Ops:
  0.0 0.0 copy-start.5
  0.0 0.7 %copy-done.5 = bf16[1,2,2,3,128]{4,2,3,1,0:T(2,128)(2,1)S(1)} copy-done((bf16[1,2,2,3,128]{4,2,3,1,0:T(2,128)(2,1)S(1)}, bf16[1,2,2,3,128]{4,2,3,1,0:T(2,128)(2,1)}, u32[]{:S(2)}) %copy-start.5) | copy-done | bytes 3096
  0.7 0.0 copy-start
  0.7 0.9 %copy-done = bf16[1,2,2,128,128]{4,3,2,1,0:T(8,128)(2,1)S(1)} copy-done((bf16[1,2,2,128,128]{4,3,2,1,0:T(8,128)(2,1)S(1)}, bf16[1,2,2,128,128]{4,3,2,1,0:T(8,128)(2,1)}, u32[]{:S(2)}) %copy-start) | copy-done | bytes 131096
  1.6 0.0 copy-start.1
  1.6 0.9 %copy-done.1 = bf16[512,128]{1,0:T(8,128)(2,1)S(1)} copy-done((bf16[512,128]{1,0:T(8,128)(2,1)S(1)}, bf16[512,128]{1,0:T(8,128)(2,1)}, u32[]{:S(2)}) %copy-start.1) | copy-done | bytes 131096
  2.5 0.0 copy-start.2
  2.5 0.8 %copy-done.2 = bf16[64,384]{1,0:T(8,128)(2,1)S(1)} copy-done((bf16[64,384]{1,0:T(8,128)(2,1)S(1)}, bf16[64,384]{1,0:T(8,128)(2,1)}, u32[]{:S(2)}) %copy-start.2) | copy-done | bytes 49176
  3.3 0.0 copy-start.3
  3.3 0.7 %copy-done.3 = s32[1,2,2,128,8]{3,4,2,1,0:T(8,128)S(1)} copy-done((s32[1,2,2,128,8]{3,4,2,1,0:T(8,128)S(1)}, s32[1,2,2,128,8]{3,4,2,1,0:T(8,128)}, u32[]{:S(2)}) %copy-start.3) | copy-done | bytes 16408
  4.0 0.0 copy-start.4
  4.0 0.7 %copy-done.4 = f32[8,64]{1,0:T(8,128)S(1)} copy-done((f32[8,64]{1,0:T(8,128)S(1)}, f32[8,64]{1,0:T(8,128)}, u32[]{:S(2)}) %copy-start.4) | copy-done | bytes 2072
  4.7 0.0 copy-start.6
  4.7 0.7 %copy-done.6 = s32[1,2,2,128]{3,2,1,0:T(2,128)S(1)} copy-done((s32[1,2,2,128]{3,2,1,0:T(2,128)S(1)}, s32[1,2,2,128]{3,2,1,0:T(2,128)}, u32[]{:S(2)}) %copy-start.6) | copy-done | bytes 2072
  5.4 0.0 copy-start.7
  5.4 0.7 %copy-done.7 = s32[1,2,2]{2,1,0:T(2,128)S(1)} copy-done((s32[1,2,2]{2,1,0:T(2,128)S(1)}, s32[1,2,2]{2,1,0:T(2,128)}, u32[]{:S(2)}) %copy-start.7) | copy-done | bytes 40
  6.1 55.2 %shard_map.82 = bf16[1,2,2,128,128]{4,3,2,1,0:T(8,128)(2,1)S(1)} custom-call(bf16[1,2,2,128,128]{4,3,2,1,0:T(8,128)(2,1)S(1)} %copy-done, bf16[1,2,3,2,128]{4,3,2,1,0:T(2,128)(2,1)S(1)} %bitcast.3, s32[1,2,2,8,128]{4,3,2,1,0:T(8,128)S(1)} %bitcast.2, s32[1,2,2,128]{3,2,1,0:T(2,128)S(1)} %copy-done.6, s32[1,2,2]{2,1,0:T(2,128)S(1)} %copy-done.7, ...), custom_call_target="tpu_custom_call" | custom-call | flops 4000000000 | bytes 4000000 | tf_op jit(solution)/shard_map/pallas_call | solution.py:383
  61.3 0.7 %copy.10 = bf16[1,2,2,128,128]{4,3,2,1,0:T(8,128)(2,1)} copy(bf16[1,2,2,128,128]{4,3,2,1,0:T(8,128)(2,1)S(1)} %shard_map.82) | data formatting | bytes 262144
Async XLA Ops:
  0.0 0.7 %copy-start.5 = (bf16[1,2,2,3,128]{4,2,3,1,0:T(2,128)(2,1)S(1)}, bf16[1,2,2,3,128]{4,2,3,1,0:T(2,128)(2,1)}, u32[]{:S(2)}) copy-start(bf16[1,2,2,3,128]{4,2,3,1,0:T(2,128)(2,1)} %param.9) | copy-start | bytes 9220
  0.7 0.9 %copy-start = (bf16[1,2,2,128,128]{4,3,2,1,0:T(8,128)(2,1)S(1)}, bf16[1,2,2,128,128]{4,3,2,1,0:T(8,128)(2,1)}, u32[]{:S(2)}) copy-start(bf16[1,2,2,128,128]{4,3,2,1,0:T(8,128)(2,1)} %feats.1) | copy-start | bytes 393220
  1.6 0.9 %copy-start.1 = (bf16[512,128]{1,0:T(8,128)(2,1)S(1)}, bf16[512,128]{1,0:T(8,128)(2,1)}, u32[]{:S(2)}) copy-start(bf16[512,128]{1,0:T(8,128)(2,1)} %mix_weight.1) | copy-start | bytes 393220
  2.5 0.8 %copy-start.2 = (bf16[64,384]{1,0:T(8,128)(2,1)S(1)}, bf16[64,384]{1,0:T(8,128)(2,1)}, u32[]{:S(2)}) copy-start(bf16[64,384]{1,0:T(8,128)(2,1)} %radial_out.1) | copy-start | bytes 147460
  3.3 0.7 %copy-start.3 = (s32[1,2,2,128,8]{3,4,2,1,0:T(8,128)S(1)}, s32[1,2,2,128,8]{3,4,2,1,0:T(8,128)}, u32[]{:S(2)}) copy-start(s32[1,2,2,128,8]{3,4,2,1,0:T(8,128)} %param.11) | copy-start | bytes 49156
  4.0 0.7 %copy-start.4 = (f32[8,64]{1,0:T(8,128)S(1)}, f32[8,64]{1,0:T(8,128)}, u32[]{:S(2)}) copy-start(f32[8,64]{1,0:T(8,128)} %radial_in.1) | copy-start | bytes 6148
  4.7 0.7 %copy-start.6 = (s32[1,2,2,128]{3,2,1,0:T(2,128)S(1)}, s32[1,2,2,128]{3,2,1,0:T(2,128)}, u32[]{:S(2)}) copy-start(s32[1,2,2,128]{3,2,1,0:T(2,128)} %pairs.1) | copy-start | bytes 6148
  5.4 0.7 %copy-start.7 = (s32[1,2,2]{2,1,0:T(2,128)S(1)}, s32[1,2,2]{2,1,0:T(2,128)}, u32[]{:S(2)}) copy-start(s32[1,2,2]{2,1,0:T(2,128)} %counts.1) | copy-start | bytes 52

commit v2 on v1

--- a/solution.py
+++ b/solution.py
@@ -35,14 +35,20 @@
 def kernel(
     sizes,
     feats,
+    offs_in,
+    lists_in,
+    pairs_in,
+    counts,
+    radial_in_in,
+    radial_out_in,
+    mix_weight_in,
+    out,
     offs,
     lists,
     pairs,
-    counts,
     radial_in,
     radial_out,
     mix_weight,
-    out,
     ext,
     places,
     hot_in,
@@ -52,8 +58,10 @@
     radial,
     gathered,
     own_sem,
+    input_sem,
     send_sem,
     recv_sem,
+    far_sem,
 ):
     size_x, size_y, size_z = sizes
     me_x, me_y, me_z = (lax.axis_index(axis) for axis in AXES)
@@ -85,39 +93,59 @@
     z_from_ext = {-1: pl.ds(1, 1), 0: pl.ds(1, 2), 1: pl.ds(2, 1)}
     z_to = {-1: pl.ds(3, 1), 0: pl.ds(1, 2), 1: pl.ds(0, 1)}
 
-    place_y = [
-        remote(0, places.at[1, 1, 2], places.at[1, 1, 0], at(0, 1, 0)),
-        remote(1, places.at[1, 1, 1], places.at[1, 1, 3], at(0, -1, 0)),
-    ]
-    feat_y = [
-        remote(2, feats.at[0, 1], ext.at[1, 0, pl.ds(1, 2)], at(0, 1, 0)),
-        remote(3, feats.at[0, 0], ext.at[1, 3, pl.ds(1, 2)], at(0, -1, 0)),
-    ]
-    place_around = [
-        remote(4 + n, places.at[1, 1], places.at[1 - dx, 1 - dz], at(dx, 0, dz))
-        for n, (dx, dz) in enumerate(AROUND)
-    ]
-    feat_own = [
-        remote(
-            12 + n,
-            feats.at[0, pl.ds(0, 2), z_from[dz]],
-            ext.at[1 - dx, pl.ds(1, 2), z_to[dz]],
-            at(dx, 0, dz),
-        )
-        for n, (dx, dz) in enumerate(AROUND)
-    ]
-
-    def feat_relay(slot):
-        row = 3 * slot
+    late = lax.rem(me_y, 2)
+    early = 1 - late
+    far_step = 2 * late - 1
+
+    def to_y(first, source, target, slot):
+        return remote(first + slot, source, target, at(0, 2 * slot - 1, 0))
+
+    def place_y(slot):
+        return to_y(0, places.at[1, 1, 1 + slot], places.at[1, 1, 3 - 3 * slot], slot)
+
+    def feat_y(slot):
+        return to_y(2, feats.at[0, slot], ext.at[1, 3 - 3 * slot, pl.ds(1, 2)], slot)
+
+    def around(first, source, target):
         return [
-            remote(
-                20 + 8 * slot + n,
-                ext.at[1, row, z_from_ext[dz]],
-                ext.at[1 - dx, row, z_to[dz]],
-                at(dx, 0, dz),
-            )
+            remote(first + n, source(dx, dz), target(dx, dz), at(dx, 0, dz))
             for n, (dx, dz) in enumerate(AROUND)
         ]
+
+    def place_early():
+        rows = pl.ds(early, 3)
+        return around(
+            4,
+            lambda dx, dz: places.at[1, 1, rows],
+            lambda dx, dz: places.at[1 - dx, 1 - dz, rows],
+        )
+
+    def place_late():
+        return around(
+            12,
+            lambda dx, dz: places.at[1, 1, 3 * late],
+            lambda dx, dz: places.at[1 - dx, 1 - dz, 3 * late],
+        )
+
+    def feat_own():
+        return around(
+            20,
+            lambda dx, dz: feats.at[0, pl.ds(0, 2), z_from[dz]],
+            lambda dx, dz: ext.at[1 - dx, pl.ds(1, 2), z_to[dz]],
+        )
+
+    def feat_relay(first, slot):
+        return around(
+            first,
+            lambda dx, dz: ext.at[1, 3 * slot, z_from_ext[dz]],
+            lambda dx, dz: ext.at[1 - dx, 3 * slot, z_to[dz]],
+        )
+
+    def feat_early():
+        return feat_relay(28, early)
+
+    def feat_late():
+        return feat_relay(36, late)
 
     def start_around(copies):
         for (dx, dz), copy in zip(AROUND, copies):
@@ -304,42 +332,94 @@
         live_slot = lax.broadcasted_iota(jnp.int32, (128, 128), 0) < counts[0, hy, hz]
         out[0, hy, hz] = jnp.where(live_slot, mixed, 0.0).astype(BF16)
 
-    def each_bin(body):
+    def each_bin(body, hy=None):
         def step(b, carry):
-            body(b)
+            body(b if hy is None else 2 * hy + b)
             return carry
 
-        lax.fori_loop(0, 4, step, 0)
+        lax.fori_loop(0, 4 if hy is None else 2, step, 0)
+
+    def greet(barrier, device):
+        pl.semaphore_signal(barrier, inc=1, device_id=device, device_id_type=MESH)
+
+    half_y = size_y // 2
+    upper = me_y // half_y
+    in_half = lax.rem(me_y, half_y)
+    at_edge = (in_half == 0) | (in_half == half_y - 1)
+    first_far, second_far = at_edge & (upper == 0), at_edge & (upper == 1)
+    idle_above = size_z - 1 - z_last
+
+    def between(pair):
+        low = pair < idle_above
+        y_first = jnp.where(upper == 0, me_y, lax.rem(me_y + far_step + size_y, size_y))
+        return (
+            me_x,
+            jnp.where(low, y_first, y_first + half_y),
+            jnp.where(low, z_last + 1 + pair, pair - idle_above),
+        )
 
     @pl.when(jnp.logical_not(live))
     def _():
         out[...] = jnp.zeros_like(out)
+        low = (upper == 0) & (me_z > z_last)
+        high = (upper == 1) & (me_z < z_first)
+
+        @pl.when(at_edge & (low | high))
+        def _():
+            barrier = pltpu.get_barrier_semaphore()
+            pair = jnp.where(low, me_z - z_last - 1, me_z + idle_above)
+            pl.semaphore_wait(barrier, 2)
+            pl.semaphore_signal(
+                far_sem,
+                inc=1,
+                device_id=(me_x, me_y - half_y * upper, z_first + pair),
+                device_id_type=MESH,
+            )
 
     @pl.when(live)
     def _():
         barrier = pltpu.get_barrier_semaphore()
-        for dy in (-1, 1):
-            pl.semaphore_signal(barrier, inc=1, device_id=at(0, dy, 0), device_id_type=MESH)
+        pl.when(at_edge)(lambda: greet(barrier, between(me_z - z_first)))
+        pl.when(jnp.logical_not(second_far))(lambda: greet(barrier, at(0, far_step, 0)))
+        greet(barrier, at(0, -far_step, 0))
         for dx, dz in AROUND:
-
-            @pl.when(has(dz))
-            def _():
-                pl.semaphore_signal(barrier, inc=1, device_id=at(dx, 0, dz), device_id_type=MESH)
-
+            pl.when(has(dz))(functools.partial(greet, barrier, at(dx, 0, dz)))
+
+        inputs = [
+            pltpu.make_async_copy(source, target, input_sem.at[n])
+            for n, (source, target) in enumerate(
+                (
+                    (offs_in, offs),
+                    (lists_in, lists),
+                    (pairs_in, pairs),
+                    (radial_in_in, radial_in),
+                    (radial_out_in, radial_out),
+                    (mix_weight_in, mix_weight),
+                )
+            )
+        ]
         own_copy = pltpu.make_async_copy(feats.at[0], ext.at[1, pl.ds(1, 2), pl.ds(1, 2)], own_sem)
+        for copy in inputs:
+            copy.start()
         own_copy.start()
+        inputs[0].wait()
         for y in range(2):
             for c in range(3):
                 value = offs[0, y, c].astype(F32)
                 for z in range(2):
                     places[1, 1, 1 + y, 3 * z + c : 3 * z + c + 1, :] = value[z : z + 1]
             places[1, 1, 1 + y, 6:8, :] = jnp.zeros((2, 128), F32)
-        pl.semaphore_wait(
-            barrier, 4 + 3 * below.astype(jnp.int32) + 3 * above.astype(jnp.int32)
-        )
-        for copy in place_y + feat_y:
-            copy.start()
-        start_around(feat_own)
+        near = 3 + 3 * below.astype(jnp.int32) + 3 * above.astype(jnp.int32)
+        pl.semaphore_wait(barrier, near + jnp.where(first_far, 0, 1))
+
+        def send_far():
+            place_y(late).start()
+            feat_y(late).start()
+
+        pl.when(jnp.logical_not(first_far))(send_far)
+        place_y(early).start()
+        feat_y(early).start()
+        start_around(feat_own())
 
         @pl.when(jnp.logical_not(below))
         def _():
@@ -349,52 +429,56 @@
         def _():
             ext[:, :, 3] = jnp.zeros((3, 4, 128, 128), BF16)
 
+        for copy in inputs[1:]:
+            copy.wait()
         each_bin(one_hots)
-        for copy in place_y:
-            copy.wait_recv()
-        start_around(place_around)
-        early = lax.rem(me_y, 2)
-
-        def relay(slot):
-            feat_y[slot].wait_recv()
-            start_around(feat_relay(slot))
-
-        pl.when(early == 0)(functools.partial(relay, 1))
-        pl.when(early == 1)(functools.partial(relay, 0))
-        recv_around(place_around)
-        each_bin(geometry)
-        pl.when(early == 0)(functools.partial(relay, 0))
-        pl.when(early == 1)(functools.partial(relay, 1))
+        place_y(1 - early).wait_recv()
+        start_around(place_early())
+        feat_y(1 - early).wait_recv()
+        start_around(feat_early())
         own_copy.wait()
-        recv_around(feat_own)
+        recv_around(feat_own())
         each_bin(gather_inner)
-        recv_around(feat_relay(0))
-        recv_around(feat_relay(1))
-        each_bin(finish)
-        for copy in place_y + feat_y:
-            copy.wait_send()
-        for copies in (place_around, feat_own, feat_relay(0), feat_relay(1)):
-            send_around(copies)
+        recv_around(place_early())
+        each_bin(geometry, early)
+        recv_around(feat_early())
+        each_bin(finish, early)
+
+        @pl.when(first_far)
+        def _():
+            pl.semaphore_wait(far_sem, 1)
+            send_far()
+
+        place_y(1 - late).wait_recv()
+        start_around(place_late())
+        feat_y(1 - late).wait_recv()
+        start_around(feat_late())
+        recv_around(place_late())
+        each_bin(geometry, late)
+        recv_around(feat_late())
+        each_bin(finish, late)
+        for slot in range(2):
+            place_y(slot).wait_send()
+            feat_y(slot).wait_send()
+        for copies in (place_early, place_late, feat_own, feat_early, feat_late):
+            send_around(copies())
 
 
 def per_device(sizes, *arrays):
     node_feats, offsets, counts, neighbours, pair_counts, radial_in, radial_out, mix_weight = arrays
-    vmem = pl.BlockSpec(memory_space=pltpu.VMEM)
+    hbm = pl.BlockSpec(memory_space=pl.ANY)
     return pl.pallas_call(
         functools.partial(kernel, sizes),
         out_shape=jax.ShapeDtypeStruct(node_feats.shape, BF16),
-        in_specs=[
-            pl.BlockSpec(memory_space=pl.ANY),
-            vmem,
-            vmem,
-            vmem,
-            pl.BlockSpec(memory_space=pltpu.SMEM),
-            vmem,
-            vmem,
-            vmem,
-        ],
-        out_specs=vmem,
+        in_specs=[hbm, hbm, hbm, hbm, pl.BlockSpec(memory_space=pltpu.SMEM), hbm, hbm, hbm],
+        out_specs=pl.BlockSpec(memory_space=pltpu.VMEM),
         scratch_shapes=[
+            pltpu.VMEM((1, 2, 3, 2, 128), BF16),
+            pltpu.VMEM((1, 2, 2, 8, 128), jnp.int32),
+            pltpu.VMEM((1, 2, 2, 128), jnp.int32),
+            pltpu.VMEM((8, 64), F32),
+            pltpu.VMEM((64, 384), BF16),
+            pltpu.VMEM((512, 128), BF16),
             pltpu.VMEM((3, 4, 4, 128, 128), BF16),
             pltpu.VMEM((3, 3, 4, 8, 128), F32),
             pltpu.VMEM((4, 1024, 1152), BF16),
@@ -404,11 +488,13 @@
             pltpu.VMEM((4, 1024, 384), BF16),
             pltpu.VMEM((4, 1024, 128), F32),
             pltpu.SemaphoreType.DMA,
-            pltpu.SemaphoreType.DMA((36,)),
-            pltpu.SemaphoreType.DMA((36,)),
+            pltpu.SemaphoreType.DMA((6,)),
+            pltpu.SemaphoreType.DMA((44,)),
+            pltpu.SemaphoreType.DMA((44,)),
+            pltpu.SemaphoreType.REGULAR,
         ],
         compiler_params=pltpu.CompilerParams(
-            collective_id=0, has_side_effects=True, vmem_limit_bytes=50 * 1024 * 1024
+            collective_id=0, has_side_effects=True, vmem_limit_bytes=63 * 1024 * 1024
         ),
         cost_estimate=pl.CostEstimate(
             flops=4_000_000_000, bytes_accessed=4_000_000, transcendentals=600_000

time: 62.3 us -> 44.6 us (0.72)
  the two profiles are of different devices: /device:TPU:160 before, /device:TPU:129 now
where the time goes in v2:
time: 44.6 us; the launch traced here: 44.4 us
  Pallas kernels  42.9 us (96%)
  local copies, waits for them, and re-layouts  1.57 us (4%)
    pallas_call x1, Pallas kernels, per_device(): pl.pallas_call(functools.partial(kernel, sizes), out_shape=jax.ShapeDtype...  42.9 us
    unnamed x1, local copies, waits for them, and re-layouts  1.57 us

profile of v2, /device:TPU:129, one launch (start us, length us, event | category | flops | bytes accessed | tf_op | source)
XLA Modules:
  0.0 44.4 jit_solution(8259785732660375787)
XLA Ops:
  0.0 42.9 %shard_map.82 = bf16[1,2,2,128,128]{4,3,2,1,0:T(8,128)(2,1)} custom-call(bf16[1,2,2,128,128]{4,3,2,1,0:T(8,128)(2,1)} %feats.1, bf16[1,2,3,2,128]{4,3,2,1,0:T(2,128)(2,1)} %bitcast.3, s32[1,2,2,8,128]{4,3,2,1,0:T(8,128)} %bitcast.2, s32[1,2,2,128]{3,2,1,0:T(2,128)} %pairs_in.1, s32[1,2,2]{2,1,0:T(2,128)} %counts.1, f32[8,64]{1,0:T(8,128)} %radial_in_in.1, ...), custom_call_target="tpu_custom_call" | custom-call | flops 4000000000 | bytes 4000000 | tf_op jit(solution)/shard_map/pallas_call | solution.py:470
  42.9 1.6 %copy.10 = bf16[1,2,2,128,128]{4,3,2,1,0:T(8,128)(2,1)} copy(bf16[1,2,2,128,128]{4,3,2,1,0:T(8,128)(2,1)} %shard_map.82) | data formatting | bytes 262144

commit v3 on v2

--- a/solution.py
+++ b/solution.py
@@ -43,6 +43,7 @@
     radial_out_in,
     mix_weight_in,
     out,
+    result,
     offs,
     lists,
     pairs,
@@ -89,8 +90,7 @@
             device_id_type=MESH,
         )
 
-    z_from = {-1: pl.ds(0, 1), 0: pl.ds(0, 2), 1: pl.ds(1, 1)}
-    z_from_ext = {-1: pl.ds(1, 1), 0: pl.ds(1, 2), 1: pl.ds(2, 1)}
+    z_from = {-1: pl.ds(1, 1), 0: pl.ds(1, 2), 1: pl.ds(2, 1)}
     z_to = {-1: pl.ds(3, 1), 0: pl.ds(1, 2), 1: pl.ds(0, 1)}
 
     late = lax.rem(me_y, 2)
@@ -104,7 +104,20 @@
         return to_y(0, places.at[1, 1, 1 + slot], places.at[1, 1, 3 - 3 * slot], slot)
 
     def feat_y(slot):
-        return to_y(2, feats.at[0, slot], ext.at[1, 3 - 3 * slot, pl.ds(1, 2)], slot)
+        return to_y(
+            2, ext.at[1, 1 + slot, pl.ds(1, 2)], ext.at[1, 3 - 3 * slot, pl.ds(1, 2)], slot
+        )
+
+    def feat_far(slot):
+        return [
+            remote(
+                46 + z,
+                ext.at[1, 1 + slot, 1 + z],
+                ext.at[1, 3 - 3 * slot, 1 + z],
+                at(0, 2 * slot - 1, 0),
+            )
+            for z in range(2)
+        ]
 
     def around(first, source, target):
         return [
@@ -130,22 +143,33 @@
     def feat_own():
         return around(
             20,
-            lambda dx, dz: feats.at[0, pl.ds(0, 2), z_from[dz]],
+            lambda dx, dz: ext.at[1, pl.ds(1, 2), z_from[dz]],
             lambda dx, dz: ext.at[1 - dx, pl.ds(1, 2), z_to[dz]],
         )
 
-    def feat_relay(first, slot):
+    def feat_early():
+        row = 3 * early
         return around(
-            first,
-            lambda dx, dz: ext.at[1, 3 * slot, z_from_ext[dz]],
-            lambda dx, dz: ext.at[1 - dx, 3 * slot, z_to[dz]],
-        )
-
-    def feat_early():
-        return feat_relay(28, early)
-
-    def feat_late():
-        return feat_relay(36, late)
+            28,
+            lambda dx, dz: ext.at[1, row, z_from[dz]],
+            lambda dx, dz: ext.at[1 - dx, row, z_to[dz]],
+        )
+
+    def feat_late(z):
+        row = 3 * late
+        side = 2 * z - 1
+        return [
+            (
+                dz,
+                remote(
+                    36 + 5 * z + n,
+                    ext.at[1, row, 1 + z],
+                    ext.at[1 - dx, row, 1 + z if dz == 0 else 3 - 3 * z],
+                    at(dx, 0, dz),
+                ),
+            )
+            for n, (dx, dz) in enumerate(((0, side), (-1, side), (1, side), (-1, 0), (1, 0)))
+        ]
 
     def start_around(copies):
         for (dx, dz), copy in zip(AROUND, copies):
@@ -180,11 +204,15 @@
         inner = (layer == 0) | (layer == 1)
         around = step_x * 3 + step_z
         t_in = jnp.where(used & inner, around, -1)
-        t_out = jnp.where(used & jnp.logical_not(inner), around, -1)
+        column = step_x == 1
+        beyond = column & (step_z == 2 * hz)
+        chunk = jnp.where(column, jnp.where(beyond, 3, 4), step_z)
+        t_out = jnp.where(used & jnp.logical_not(inner), chunk, -1)
+        side = jnp.where(column, jnp.where(beyond, 0, step_z - 1 + hz), step_x >> 1)
         slot_col = slot.astype(F32).T
         in_col = t_in.astype(F32).T
         out_col = t_out.astype(F32).T
-        halves[b] = layer.astype(F32).T
+        halves[b] = jnp.where(inner, layer, side).astype(F32).T
         lanes = lax.broadcasted_iota(jnp.int32, (128, 128), 1).astype(F32).astype(BF16)
         zero = jnp.zeros((128, 128), BF16)
         for k in range(8):
@@ -198,7 +226,8 @@
             for t in range(9):
                 cols = pl.ds(128 * t, 128)
                 hot_in[b, rows, cols] = jnp.where(in_k == float(t), slots, zero)
-                hot_out[b, rows, cols] = jnp.where(out_k == float(t), slots, zero)
+                if t < 5:
+                    hot_out[b, rows, cols] = jnp.where(out_k == float(t), slots, zero)
 
     def geometry(b):
         hy, hz = b // 2, b % 2
@@ -273,28 +302,49 @@
                     )
                     spread[b, group, pl.ds(32 * m, 32), pl.ds(128 * part, 128)] = block.astype(BF16)
 
+    def pick_half(b, both, k):
+        part = both[128 * k : 128 * (k + 1)]
+        upper = jnp.broadcast_to(halves[b, :, k : k + 1], (128, 128)) > 0.5
+        return jnp.where(upper, part[:, 128:], part[:, :128])
+
+    def pair_up(pairs_of_bins):
+        return jnp.concatenate(
+            [jnp.concatenate([ext[first], ext[second]], axis=1) for first, second in pairs_of_bins],
+            axis=0,
+        )
+
+    def out_copy(hy, hz):
+        return pltpu.make_async_copy(
+            result.at[0, hy, hz], out.at[0, hy, hz], input_sem.at[2 * hy + hz]
+        )
+
     def gather_inner(b):
         hz = b % 2
-        table = jnp.concatenate(
-            [
-                jnp.concatenate([ext[dx, 1, hz + dz], ext[dx, 2, hz + dz]], axis=1)
-                for dx in range(3)
-                for dz in range(3)
-            ],
-            axis=0,
+        table = pair_up(
+            [((dx, 1, hz + dz), (dx, 2, hz + dz)) for dx in range(3) for dz in range(3)]
         )
         both = jnp.dot(hot_in[b], table, preferred_element_type=F32)
         for k in range(8):
-            part = both[128 * k : 128 * (k + 1)]
-            upper = jnp.broadcast_to(halves[b, :, k : k + 1], (128, 128)) > 0.5
-            gathered[b, pl.ds(128 * k, 128)] = jnp.where(upper, part[:, 128:], part[:, :128])
+            gathered[b, pl.ds(128 * k, 128)] = pick_half(b, both, k)
+
+    def gather_column(b):
+        row = 3 * (b // 2)
+        table = pair_up([((1, row, 1), (1, row, 2))])
+        both = jnp.dot(hot_out[b, :, pl.ds(512, 128)], table, preferred_element_type=F32)
+        for k in range(8):
+            gathered[b, pl.ds(128 * k, 128)] += pick_half(b, both, k)
 
     def finish(b):
         hy, hz = b // 2, b % 2
-        table = jnp.concatenate(
-            [ext[dx, 3 * hy, hz + dz] for dx in range(3) for dz in range(3)], axis=0
-        )
-        theirs = gathered[b] + jnp.dot(hot_out[b], table, preferred_element_type=F32)
+        row = 3 * hy
+        table = pair_up(
+            [((0, row, hz + dz), (2, row, hz + dz)) for dz in range(3)]
+            + [((1, row, 3 * hz), (1, row, 3 * hz))]
+        )
+        both = jnp.dot(hot_out[b, :, pl.ds(0, 512)], table, preferred_element_type=F32)
+        theirs = jnp.concatenate(
+            [gathered[b, pl.ds(128 * k, 128)] + pick_half(b, both, k) for k in range(8)], axis=0
+        )
         first = radial[b, :, 0:128].astype(F32) * theirs
         total = first[0:128]
         for k in range(1, 8):
@@ -330,7 +380,8 @@
         )
         mixed = jnp.dot(joined, mix_weight[...], preferred_element_type=F32)
         live_slot = lax.broadcasted_iota(jnp.int32, (128, 128), 0) < counts[0, hy, hz]
-        out[0, hy, hz] = jnp.where(live_slot, mixed, 0.0).astype(BF16)
+        result[0, hy, hz] = jnp.where(live_slot, mixed, 0.0).astype(BF16)
+        out_copy(hy, hz).start()
 
     def each_bin(body, hy=None):
         def step(b, carry):
@@ -360,7 +411,9 @@
 
     @pl.when(jnp.logical_not(live))
     def _():
-        out[...] = jnp.zeros_like(out)
+        result[...] = jnp.zeros_like(result)
+        copy = pltpu.make_async_copy(result, out, own_sem)
+        copy.start()
         low = (upper == 0) & (me_z > z_last)
         high = (upper == 1) & (me_z < z_first)
 
@@ -375,6 +428,8 @@
                 device_id=(me_x, me_y - half_y * upper, z_first + pair),
                 device_id_type=MESH,
             )
+
+        copy.wait()
 
     @pl.when(live)
     def _():
@@ -399,9 +454,9 @@
             )
         ]
         own_copy = pltpu.make_async_copy(feats.at[0], ext.at[1, pl.ds(1, 2), pl.ds(1, 2)], own_sem)
+        own_copy.start()
         for copy in inputs:
             copy.start()
-        own_copy.start()
         inputs[0].wait()
         for y in range(2):
             for c in range(3):
@@ -409,17 +464,23 @@
                 for z in range(2):
                     places[1, 1, 1 + y, 3 * z + c : 3 * z + c + 1, :] = value[z : z + 1]
             places[1, 1, 1 + y, 6:8, :] = jnp.zeros((2, 128), F32)
+        own_copy.wait()
         near = 3 + 3 * below.astype(jnp.int32) + 3 * above.astype(jnp.int32)
         pl.semaphore_wait(barrier, near + jnp.where(first_far, 0, 1))
 
         def send_far():
             place_y(late).start()
-            feat_y(late).start()
+            for copy in feat_far(late):
+                copy.start()
+
+        def greeted():
+            pl.semaphore_wait(far_sem, 1)
+            send_far()
 
         pl.when(jnp.logical_not(first_far))(send_far)
         place_y(early).start()
         feat_y(early).start()
-        start_around(feat_own())
+        pl.when(jnp.logical_not(second_far))(lambda: start_around(feat_own()))
 
         @pl.when(jnp.logical_not(below))
         def _():
@@ -432,36 +493,50 @@
         for copy in inputs[1:]:
             copy.wait()
         each_bin(one_hots)
+
+        @pl.when(second_far)
+        def _():
+            start_around(feat_own())
+
         place_y(1 - early).wait_recv()
         start_around(place_early())
         feat_y(1 - early).wait_recv()
         start_around(feat_early())
-        own_copy.wait()
+        recv_around(place_early())
+        each_bin(geometry, early)
         recv_around(feat_own())
         each_bin(gather_inner)
-        recv_around(place_early())
-        each_bin(geometry, early)
+        each_bin(gather_column, early)
+        soon = me_z - z_first >= size_z // 4
+        pl.when(first_far & soon)(greeted)
         recv_around(feat_early())
         each_bin(finish, early)
-
-        @pl.when(first_far)
-        def _():
-            pl.semaphore_wait(far_sem, 1)
-            send_far()
-
+        pl.when(first_far & jnp.logical_not(soon))(greeted)
         place_y(1 - late).wait_recv()
         start_around(place_late())
-        feat_y(1 - late).wait_recv()
-        start_around(feat_late())
+        for z, copy in enumerate(feat_far(1 - late)):
+            copy.wait_recv()
+            for dz, onward in feat_late(z):
+                pl.when(has(dz))(onward.start)
+        each_bin(gather_column, late)
         recv_around(place_late())
         each_bin(geometry, late)
-        recv_around(feat_late())
+        for z in range(2):
+            for dz, onward in feat_late(z):
+                pl.when(has(-dz))(onward.wait_recv)
         each_bin(finish, late)
-        for slot in range(2):
-            place_y(slot).wait_send()
-            feat_y(slot).wait_send()
-        for copies in (place_early, place_late, feat_own, feat_early, feat_late):
+        place_y(0).wait_send()
+        place_y(1).wait_send()
+        feat_y(early).wait_send()
+        for copy in feat_far(late):
+            copy.wait_send()
+        for copies in (place_early, place_late, feat_own, feat_early):
             send_around(copies())
+        for z in range(2):
+            for dz, onward in feat_late(z):
+                pl.when(has(dz))(onward.wait_send)
+        for b in range(4):
+            out_copy(b // 2, b % 2).wait()
 
 
 def per_device(sizes, *arrays):
@@ -471,8 +546,9 @@
         functools.partial(kernel, sizes),
         out_shape=jax.ShapeDtypeStruct(node_feats.shape, BF16),
         in_specs=[hbm, hbm, hbm, hbm, pl.BlockSpec(memory_space=pltpu.SMEM), hbm, hbm, hbm],
-        out_specs=pl.BlockSpec(memory_space=pltpu.VMEM),
+        out_specs=hbm,
         scratch_shapes=[
+            pltpu.VMEM((1, 2, 2, 128, 128), BF16),
             pltpu.VMEM((1, 2, 3, 2, 128), BF16),
             pltpu.VMEM((1, 2, 2, 8, 128), jnp.int32),
             pltpu.VMEM((1, 2, 2, 128), jnp.int32),
@@ -482,15 +558,15 @@
             pltpu.VMEM((3, 4, 4, 128, 128), BF16),
             pltpu.VMEM((3, 3, 4, 8, 128), F32),
             pltpu.VMEM((4, 1024, 1152), BF16),
-            pltpu.VMEM((4, 1024, 1152), BF16),
+            pltpu.VMEM((4, 1024, 640), BF16),
             pltpu.VMEM((4, 128, 8), F32),
             pltpu.VMEM((4, 4, 256, 256), BF16),
             pltpu.VMEM((4, 1024, 384), BF16),
             pltpu.VMEM((4, 1024, 128), F32),
             pltpu.SemaphoreType.DMA,
             pltpu.SemaphoreType.DMA((6,)),
-            pltpu.SemaphoreType.DMA((44,)),
-            pltpu.SemaphoreType.DMA((44,)),
+            pltpu.SemaphoreType.DMA((48,)),
+            pltpu.SemaphoreType.DMA((48,)),
             pltpu.SemaphoreType.REGULAR,
         ],
         compiler_params=pltpu.CompilerParams(

time: 44.6 us -> 43.5 us (0.975)
  the two profiles are of different devices: /device:TPU:129 before, /device:TPU:128 now
where the time goes in v3:
time: 43.5 us; the launch traced here: 43.3 us
  Pallas kernels  41.7 us (96%)
  local copies, waits for them, and re-layouts  1.57 us (4%)
    pallas_call x1, Pallas kernels, per_device(): pl.pallas_call(functools.partial(kernel, sizes), out_shape=jax.ShapeDtype...  41.7 us
    unnamed x1, local copies, waits for them, and re-layouts  1.57 us

profile of v3, /device:TPU:128, one launch (start us, length us, event | category | flops | bytes accessed | tf_op | source)
XLA Modules:
  0.0 43.3 jit_solution(18420985952932498345)
XLA Ops:
  0.0 41.7 %shard_map.82 = bf16[1,2,2,128,128]{4,3,2,1,0:T(8,128)(2,1)} custom-call(bf16[1,2,2,128,128]{4,3,2,1,0:T(8,128)(2,1)} %feats.1, bf16[1,2,3,2,128]{4,3,2,1,0:T(2,128)(2,1)} %bitcast.3, s32[1,2,2,8,128]{4,3,2,1,0:T(8,128)} %bitcast.2, s32[1,2,2,128]{3,2,1,0:T(2,128)} %pairs_in.1, s32[1,2,2]{2,1,0:T(2,128)} %counts.1, f32[8,64]{1,0:T(8,128)} %radial_in_in.1, ...), custom_call_target="tpu_custom_call" | custom-call | flops 4000000000 | bytes 4000000 | tf_op jit(solution)/shard_map/pallas_call | solution.py:545
  41.7 1.6 %copy.10 = bf16[1,2,2,128,128]{4,3,2,1,0:T(8,128)(2,1)} copy(bf16[1,2,2,128,128]{4,3,2,1,0:T(8,128)(2,1)} %shard_map.82) | data formatting | bytes 262144

commit v4 on v3

--- a/solution.py
+++ b/solution.py
@@ -15,7 +15,7 @@
 FLOOR_BINS = 0.25
 AXES = ("gx", "gy", "gz")
 MESH = pl.DeviceIdType.MESH
-AROUND = [(dx, dz) for dz in (-1, 0, 1) for dx in (-1, 0, 1) if (dx, dz) != (0, 0)]
+AROUND = [(-1, -1), (1, -1), (-1, 1), (1, 1), (0, -1), (0, 1), (-1, 0), (1, 0)]
 BF16 = jnp.bfloat16
 F32 = jnp.float32
 
@@ -108,17 +108,6 @@
             2, ext.at[1, 1 + slot, pl.ds(1, 2)], ext.at[1, 3 - 3 * slot, pl.ds(1, 2)], slot
         )
 
-    def feat_far(slot):
-        return [
-            remote(
-                46 + z,
-                ext.at[1, 1 + slot, 1 + z],
-                ext.at[1, 3 - 3 * slot, 1 + z],
-                at(0, 2 * slot - 1, 0),
-            )
-            for z in range(2)
-        ]
-
     def around(first, source, target):
         return [
             remote(first + n, source(dx, dz), target(dx, dz), at(dx, 0, dz))
@@ -147,29 +136,18 @@
             lambda dx, dz: ext.at[1 - dx, pl.ds(1, 2), z_to[dz]],
         )
 
-    def feat_early():
-        row = 3 * early
+    def feat_relay(first, row):
         return around(
-            28,
+            first,
             lambda dx, dz: ext.at[1, row, z_from[dz]],
             lambda dx, dz: ext.at[1 - dx, row, z_to[dz]],
         )
 
-    def feat_late(z):
-        row = 3 * late
-        side = 2 * z - 1
-        return [
-            (
-                dz,
-                remote(
-                    36 + 5 * z + n,
-                    ext.at[1, row, 1 + z],
-                    ext.at[1 - dx, row, 1 + z if dz == 0 else 3 - 3 * z],
-                    at(dx, 0, dz),
-                ),
-            )
-            for n, (dx, dz) in enumerate(((0, side), (-1, side), (1, side), (-1, 0), (1, 0)))
-        ]
+    def feat_early():
+        return feat_relay(28, 3 * early)
+
+    def feat_late():
+        return feat_relay(36, 3 * late)
 
     def start_around(copies):
         for (dx, dz), copy in zip(AROUND, copies):
@@ -470,8 +448,7 @@
 
         def send_far():
             place_y(late).start()
-            for copy in feat_far(late):
-                copy.start()
+            feat_y(late).start()
 
         def greeted():
             pl.semaphore_wait(far_sem, 1)
@@ -512,29 +489,49 @@
         recv_around(feat_early())
         each_bin(finish, early)
         pl.when(first_far & jnp.logical_not(soon))(greeted)
+        place_y(early).wait_send()
+        feat_y(early).wait_send()
+        for copies in (place_early, feat_own, feat_early):
+            send_around(copies())
         place_y(1 - late).wait_recv()
         start_around(place_late())
-        for z, copy in enumerate(feat_far(1 - late)):
-            copy.wait_recv()
-            for dz, onward in feat_late(z):
-                pl.when(has(dz))(onward.start)
+        feat_y(1 - late).wait_recv()
+        start_around(feat_late())
         each_bin(gather_column, late)
-        recv_around(place_late())
-        each_bin(geometry, late)
-        for z in range(2):
-            for dz, onward in feat_late(z):
-                pl.when(has(-dz))(onward.wait_recv)
-        each_bin(finish, late)
-        place_y(0).wait_send()
-        place_y(1).wait_send()
-        feat_y(early).wait_send()
-        for copy in feat_far(late):
-            copy.wait_send()
-        for copies in (place_early, place_late, feat_own, feat_early):
-            send_around(copies())
-        for z in range(2):
-            for dz, onward in feat_late(z):
-                pl.when(has(dz))(onward.wait_send)
+        first_hz = jnp.where(above, 0, 1)
+
+        def recv_from(copies, step, also):
+            for (_, dz), copy in zip(AROUND, copies()):
+                if dz == step:
+                    pl.when(has(-dz) & also)(copy.wait_recv)
+
+        def recv_first(copies):
+            recv_from(copies, 0, live)
+            recv_from(copies, 1, above)
+
+        def recv_second(copies):
+            recv_from(copies, 1, jnp.logical_not(above))
+            recv_from(copies, -1, live)
+
+        def last_bins(t, carry):
+            b = 2 * late + jnp.where(t == 0, first_hz, 1 - first_hz)
+            pl.when(t == 0)(lambda: recv_first(place_late))
+            pl.when(t == 1)(lambda: recv_second(place_late))
+            geometry(b)
+            pl.when(t == 0)(lambda: recv_first(feat_late))
+
+            @pl.when(t == 1)
+            def _():
+                place_y(late).wait_send()
+                feat_y(late).wait_send()
+                send_around(place_late())
+                recv_second(feat_late)
+                send_around(feat_late())
+
+            finish(b)
+            return carry
+
+        lax.fori_loop(0, 2, last_bins, 0)
         for b in range(4):
             out_copy(b // 2, b % 2).wait()
 
@@ -565,8 +562,8 @@
             pltpu.VMEM((4, 1024, 128), F32),
             pltpu.SemaphoreType.DMA,
             pltpu.SemaphoreType.DMA((6,)),
-            pltpu.SemaphoreType.DMA((48,)),
-            pltpu.SemaphoreType.DMA((48,)),
+            pltpu.SemaphoreType.DMA((44,)),
+            pltpu.SemaphoreType.DMA((44,)),
             pltpu.SemaphoreType.REGULAR,
         ],
         compiler_params=pltpu.CompilerParams(

time: 43.5 us -> 42.2 us (0.970)
  the two profiles are of different devices: /device:TPU:128 before, /device:TPU:160 now
where the time goes in v4:
time: 42.2 us; the launch traced here: 42.1 us
  Pallas kernels  40.5 us (96%)
  local copies, waits for them, and re-layouts  1.57 us (4%)
    pallas_call x1, Pallas kernels, per_device(): pl.pallas_call(functools.partial(kernel, sizes), out_shape=jax.ShapeDtype...  40.5 us
    unnamed x1, local copies, waits for them, and re-layouts  1.57 us

profile of v4, /device:TPU:160, one launch (start us, length us, event | category | flops | bytes accessed | tf_op | source)
XLA Modules:
  0.0 42.1 jit_solution(5533851118913095756)
XLA Ops:
  0.0 40.5 %shard_map.82 = bf16[1,2,2,128,128]{4,3,2,1,0:T(8,128)(2,1)} custom-call(bf16[1,2,2,128,128]{4,3,2,1,0:T(8,128)(2,1)} %feats.1, bf16[1,2,3,2,128]{4,3,2,1,0:T(2,128)(2,1)} %bitcast.3, s32[1,2,2,8,128]{4,3,2,1,0:T(8,128)} %bitcast.2, s32[1,2,2,128]{3,2,1,0:T(2,128)} %pairs_in.1, s32[1,2,2]{2,1,0:T(2,128)} %counts.1, f32[8,64]{1,0:T(8,128)} %radial_in_in.1, ...), custom_call_target="tpu_custom_call" | custom-call | flops 4000000000 | bytes 4000000 | tf_op jit(solution)/shard_map/pallas_call | solution.py:542
  40.5 1.6 %copy.10 = bf16[1,2,2,128,128]{4,3,2,1,0:T(8,128)(2,1)} copy(bf16[1,2,2,128,128]{4,3,2,1,0:T(8,128)(2,1)} %shard_map.82) | data formatting | bytes 262144

commit v5 on v4

--- a/solution.py
+++ b/solution.py
@@ -43,7 +43,6 @@
     radial_out_in,
     mix_weight_in,
     out,
-    result,
     offs,
     lists,
     pairs,
@@ -289,11 +288,6 @@
         return jnp.concatenate(
             [jnp.concatenate([ext[first], ext[second]], axis=1) for first, second in pairs_of_bins],
             axis=0,
-        )
-
-    def out_copy(hy, hz):
-        return pltpu.make_async_copy(
-            result.at[0, hy, hz], out.at[0, hy, hz], input_sem.at[2 * hy + hz]
         )
 
     def gather_inner(b):
@@ -358,8 +352,7 @@
         )
         mixed = jnp.dot(joined, mix_weight[...], preferred_element_type=F32)
         live_slot = lax.broadcasted_iota(jnp.int32, (128, 128), 0) < counts[0, hy, hz]
-        result[0, hy, hz] = jnp.where(live_slot, mixed, 0.0).astype(BF16)
-        out_copy(hy, hz).start()
+        out[0, hy, hz] = jnp.where(live_slot, mixed, 0.0).astype(BF16)
 
     def each_bin(body, hy=None):
         def step(b, carry):
@@ -389,9 +382,7 @@
 
     @pl.when(jnp.logical_not(live))
     def _():
-        result[...] = jnp.zeros_like(result)
-        copy = pltpu.make_async_copy(result, out, own_sem)
-        copy.start()
+        out[...] = jnp.zeros_like(out)
         low = (upper == 0) & (me_z > z_last)
         high = (upper == 1) & (me_z < z_first)
 
@@ -406,8 +397,6 @@
                 device_id=(me_x, me_y - half_y * upper, z_first + pair),
                 device_id_type=MESH,
             )
-
-        copy.wait()
 
     @pl.when(live)
     def _():
@@ -532,20 +521,17 @@
             return carry
 
         lax.fori_loop(0, 2, last_bins, 0)
-        for b in range(4):
-            out_copy(b // 2, b % 2).wait()
 
 
 def per_device(sizes, *arrays):
     node_feats, offsets, counts, neighbours, pair_counts, radial_in, radial_out, mix_weight = arrays
-    hbm = pl.BlockSpec(memory_space=pl.ANY)
+    hbm = pl.BlockSpec(memory_space=pltpu.HBM)
     return pl.pallas_call(
         functools.partial(kernel, sizes),
-        out_shape=jax.ShapeDtypeStruct(node_feats.shape, BF16),
+        out_shape=pltpu.VMEM(node_feats.shape, BF16),
         in_specs=[hbm, hbm, hbm, hbm, pl.BlockSpec(memory_space=pltpu.SMEM), hbm, hbm, hbm],
-        out_specs=hbm,
+        out_specs=pl.BlockSpec(memory_space=pltpu.VMEM),
         scratch_shapes=[
-            pltpu.VMEM((1, 2, 2, 128, 128), BF16),
             pltpu.VMEM((1, 2, 3, 2, 128), BF16),
             pltpu.VMEM((1, 2, 2, 8, 128), jnp.int32),
             pltpu.VMEM((1, 2, 2, 128), jnp.int32),
@@ -567,7 +553,7 @@
             pltpu.SemaphoreType.REGULAR,
         ],
         compiler_params=pltpu.CompilerParams(
-            collective_id=0, has_side_effects=True, vmem_limit_bytes=63 * 1024 * 1024
+            collective_id=0, has_side_effects=True, vmem_limit_bytes=65344 * 1024
         ),
         cost_estimate=pl.CostEstimate(
             flops=4_000_000_000, bytes_accessed=4_000_000, transcendentals=600_000

time: 42.2 us -> 40.7 us (0.964)
  local copies, waits for them, and re-layouts: 1.57 us -> 0.66 us
  Pallas kernels: 40.5 us -> 39.9 us
    unnamed x1, local copies, waits for them, and re-layouts: 1.57 us -> 0.66 us
    pallas_call x1, Pallas kernels: 40.5 us -> 39.9 us  [per_device(): pl.pallas_call(functools.partial(kernel, sizes), out_shape=pltpu.VMEM(nod...]
where the time goes in v5:
time: 40.7 us; the launch traced here: 40.6 us
  Pallas kernels  39.9 us (98%)
  local copies, waits for them, and re-layouts  0.66 us (2%)
    pallas_call x1, Pallas kernels, per_device(): pl.pallas_call(functools.partial(kernel, sizes), out_shape=pltpu.VMEM(nod...  39.9 us

profile of v5, /device:TPU:160, one launch (start us, length us, event | category | flops | bytes accessed | tf_op | source)
XLA Modules:
  0.0 40.6 jit_solution(15336986253451714809)
XLA Ops:
  0.0 39.9 %shard_map.82 = bf16[1,2,2,128,128]{4,3,2,1,0:T(8,128)(2,1)S(1)} custom-call(bf16[1,2,2,128,128]{4,3,2,1,0:T(8,128)(2,1)} %feats.1, bf16[1,2,3,2,128]{4,3,2,1,0:T(2,128)(2,1)} %bitcast.3, s32[1,2,2,8,128]{4,3,2,1,0:T(8,128)} %bitcast.2, s32[1,2,2,128]{3,2,1,0:T(2,128)} %pairs_in.1, s32[1,2,2]{2,1,0:T(2,128)} %counts.1, f32[8,64]{1,0:T(8,128)} %radial_in_in.1, ...), custom_call_target="tpu_custom_call" | custom-call | flops 4000000000 | bytes 4000000 | tf_op jit(solution)/shard_map/pallas_call | solution.py:529
  39.9 0.7 %copy.10 = bf16[1,2,2,128,128]{4,3,2,1,0:T(8,128)(2,1)} copy(bf16[1,2,2,128,128]{4,3,2,1,0:T(8,128)(2,1)S(1)} %shard_map.82) | data formatting | bytes 262144
